TPU v7x, 32 devices: a whole 2x2x4 slice. The times are simulated.
32 devices in a mesh: shot: 4 (over z), space: 8 (over y, x, core).
Axes of the slice: x: 2, y: 2, z: 4, core: 2. Of those that a mesh axis runs over, the one named last changes fastest.
Arguments:
- courant: float32 [32, 256, 128], P('space'), may hold values from 0.02 to 0.18
- adjoint_now: float32 [4, 32, 256, 128], P('shot', 'space'), may hold values from -6 to 6
- adjoint_old: float32 [4, 32, 256, 128], P('shot', 'space'), may hold values from -6 to 6
- receiver_slab: int32 [4, 3072, 1], P('shot', 'space'), may hold values from 0 to 7; in each aligned block of 384 rows (0 to 383, 384 to 767, ..., all dimensions but the last counted through in order) at most 48 rows name the same one
- receiver_cell: int32 [4, 3072], P('shot', 'space'), may hold values from 0 to 131071
- residuals: float32 [4, 3, 3072], P('shot', None, 'space'), may hold values from -24 to 24
- forward_field: bfloat16 [4, 3, 32, 256, 128], P('shot', None, 'space'), may hold values from -6 to 6
Outputs:
- adjoint_last: float32 [4, 32, 256, 128], P('shot', 'space')
- adjoint_prior: float32 [4, 32, 256, 128], P('shot', 'space')
- gradient_image: float32 [32, 256, 128], P('space', 'shot')
Inputs may be any that keep to these rules, and one draw needn't show every extreme that they name: `receiver_slab`: in each aligned block of 384 receivers (those held by one index of space) at most 48 lie in one slab, and some block reaches 48.
All inputs are finite; a program needn't handle non-finite values.
Results may differ from a plain program's by a relative error of at most 0.0003.
Values sent between devices are 32-bit elements; how exact they have to be, the bound alone decides.
A program may use at most 64 MiB of HBM per device.

v0:
```python
import jax
import jax.numpy as jnp
from jax import lax
from jax.sharding import PartitionSpec as P

STEPS = 3
CAP = 48


STENCIL_WEIGHTS = (-205.0 / 72.0, 8.0 / 5.0, -1.0 / 5.0, 8.0 / 315.0, -1.0 / 560.0)


def with_halo(block, sides, width):
    for axis, dim in sides:
        count = lax.axis_size(axis)
        forward = [(i, i + 1) for i in range(count - 1)]
        backward = [(target, source) for source, target in forward]
        low = lax.ppermute(
            lax.slice_in_dim(block, block.shape[dim] - width, None, axis=dim), axis, forward
        )
        high = lax.ppermute(lax.slice_in_dim(block, 0, width, axis=dim), axis, backward)
        block = jnp.concatenate([low, block, high], axis=dim)
    return block


def laplace(padded, extent_x, extent_y, extent_z):
    center = padded[4 : 4 + extent_x, 4 : 4 + extent_y, 4 : 4 + extent_z]
    summed = 3.0 * STENCIL_WEIGHTS[0] * center
    for offset in range(1, 5):
        along = padded[4 + offset : 4 + offset + extent_x, 4 : 4 + extent_y, 4 : 4 + extent_z]
        along = (
            along + padded[4 - offset : 4 - offset + extent_x, 4 : 4 + extent_y, 4 : 4 + extent_z]
        )
        along = (
            along + padded[4 : 4 + extent_x, 4 + offset : 4 + offset + extent_y, 4 : 4 + extent_z]
        )
        along = (
            along + padded[4 : 4 + extent_x, 4 - offset : 4 - offset + extent_y, 4 : 4 + extent_z]
        )
        along = (
            along + padded[4 : 4 + extent_x, 4 : 4 + extent_y, 4 + offset : 4 + offset + extent_z]
        )
        along = (
            along + padded[4 : 4 + extent_x, 4 : 4 + extent_y, 4 - offset : 4 - offset + extent_z]
        )
        summed = summed + STENCIL_WEIGHTS[offset] * along
    return summed


def local(
    courant, adjoint_now, adjoint_old, receiver_slab, receiver_cell, residuals, forward_field
):
    extent_x, extent_y, extent_z = courant.shape
    slab_count = lax.axis_size("space")
    slab_ids = receiver_slab[0, :, 0]
    cell_ids = receiver_cell[0]
    trace_rows = residuals[0]
    onehot = (slab_ids[:, None] == jnp.arange(slab_count, dtype=jnp.int32)[None, :]).astype(
        jnp.int32
    )
    before = jnp.cumsum(onehot, axis=0) - onehot
    bucket_rank = jnp.sum(before * onehot, axis=1)
    slot_ids = slab_ids * CAP + bucket_rank
    send_values = (
        jnp.zeros((trace_rows.shape[0], slab_count * CAP), jnp.float32)
        .at[:, slot_ids]
        .set(trace_rows)
    )
    send_cells = jnp.zeros((1, slab_count * CAP), jnp.int32).at[0, slot_ids].set(cell_ids)
    got_values, got_cells = (
        lax.all_to_all(send_values, "space", split_axis=1, concat_axis=1, tiled=True),
        lax.all_to_all(send_cells, "space", split_axis=1, concat_axis=1, tiled=True),
    )
    here_cells = got_cells[0]
    current = adjoint_now[0]
    previous = adjoint_old[0]
    image_acc = jnp.zeros((extent_x, extent_y, extent_z), jnp.float32)
    for step_index in range(STEPS):
        source = (
            jnp.zeros((extent_x * extent_y * extent_z,), jnp.float32)
            .at[here_cells]
            .add(got_values[step_index])
        )
        source = source.reshape(extent_x, extent_y, extent_z)
        extended = with_halo(current, (("space", 0),), 4)
        padded = jnp.pad(extended, ((0, 0), (4, 4), (4, 4)))
        advanced = (
            2.0 * current
            - previous
            + courant * (laplace(padded, extent_x, extent_y, extent_z) + source)
        )
        image_acc = image_acc + forward_field[0, step_index].astype(jnp.float32) * advanced
        previous, current = (current, advanced)
    image_rows = lax.psum_scatter(image_acc, "shot", scatter_dimension=1, tiled=True)
    return (current[None], previous[None], image_rows)


def solution(mesh):
    in_specs = (
        P("space", None, None),
        P("shot", "space", None, None),
        P("shot", "space", None, None),
        P("shot", "space", None),
        P("shot", "space"),
        P("shot", None, "space"),
        P("shot", None, "space", None, None),
    )
    out_specs = (
        P("shot", "space", None, None),
        P("shot", "space", None, None),
        P("space", "shot", None),
    )
    return jax.shard_map(local, mesh=mesh, in_specs=in_specs, out_specs=out_specs, check_vma=False)
```

profile of v0, /device:TPU:0, one launch (start us, length us, event | category | flops | bytes accessed | tf_op | source)
XLA Modules:
  0.0 113.8 jit_solution(4923272790011542542)
XLA Ops:
  7.2 0.0 copy-start
  7.2 2.5 %collective-permute-start.1 = (f32[4,256,128]{2,1,0:T(8,128)}, f32[4,256,128]{2,1,0:T(8,128)S(1)}, u32[]{:S(2)}, u32[]{:S(2)}) collective-permute-start(f32[4,256,128]{2,1,0:T(8,128)} %bitcast.45), channel_id=1, source_target_pairs={{0,1},{1,2},{2,3},{3,4},{4,5},{5,6},{6,7},{8,9},{9,10},{10,11},{11... | collective-permute-start | bytes 1572872 | tf_op jit(solution)/shard_map/ppermute | solution.py:18
  9.7 1.3 %collective-permute-start = (f32[4,256,128]{2,1,0:T(8,128)}, f32[4,256,128]{2,1,0:T(8,128)S(1)}, u32[]{:S(2)}, u32[]{:S(2)}) collective-permute-start(f32[4,256,128]{2,1,0:T(8,128)} %bitcast.46), channel_id=1, source_target_pairs={{1,0},{2,1},{3,2},{4,3},{5,4},{6,5},{7,6},{9,8},{10,9},{11,10},{12... | collective-permute-start | bytes 1572872 | tf_op jit(solution)/shard_map/ppermute | solution.py:21
  11.0 0.7 reduce
  11.7 0.7 reduce.4
  12.4 0.9 reduce-window.6
  13.3 0.2 slice_reduce_fusion
  13.5 0.1 fusion.92
  13.6 0.7 fusion.94
  14.3 2.9 %scatter_custom_fusion = s32[384]{0:T(512)S(1)} fusion(s32[384]{0:T(512)S(1)} %fusion.94, s32[384]{0:T(512)S(1)} %reduce.4, s32[]{:T(128)} %constant.6.clone.1), kind=kCustom, calls=%fused_computation.180 | custom fusion | bytes 1540 | tf_op jit(solution)/shard_map/scatter | solution.py:69
  17.3 0.7 all_to_all.12
  17.9 7.1 %all-to-all-start = ((s32[1,8,48]{2,0,1:T(1,128)}), s32[1,8,48]{2,0,1:T(1,128)S(1)}, u32[]{:S(2)}, u32[]{:S(2)}) async-start(s32[1,8,48]{2,0,1:T(1,128)} %all_to_all.12), calls=%async_computation | async-start | bytes 8192 | tf_op jit(solution)/shard_map/all_to_all | solution.py:72
  25.0 0.7 copy.17
  25.7 0.1 copy.13
  25.8 1.5 %scatter_custom_fusion.1 = f32[3,384]{0,1:T(8,128)S(1)} fusion(s32[384]{0:T(512)S(1)} %fusion.94, f32[384,3]{1,0:T(8,128)S(1)} %copy.13, f32[]{:T(128)} %constant.13.clone.1), kind=kCustom, calls=%fused_computation.162 | custom fusion | bytes 4612 | tf_op jit(solution)/shard_map/scatter | solution.py:67
  27.3 0.1 copy.14
  27.4 0.7 reshape.197
  28.2 1.4 %all-to-all-done = s32[1,8,48]{2,0,1:T(1,128)S(1)} async-done(((s32[1,8,48]{2,0,1:T(1,128)}), s32[1,8,48]{2,0,1:T(1,128)S(1)}, u32[]{:S(2)}, u32[]{:S(2)}) %all-to-all-start) | async-done | bytes 1568 | tf_op jit(solution)/shard_map/all_to_all | solution.py:72
  29.6 3.3 %all-to-all-start.1 = ((f32[8,1,144]{2,1,0:T(1,128)}), f32[8,1,144]{2,1,0:T(1,128)S(1)}, u32[]{:S(2)}, u32[]{:S(2)}) async-start(f32[8,1,144]{2,1,0:T(1,128)} %reshape.197), calls=%async_computation.1 | async-start | bytes 16384 | tf_op jit(solution)/shard_map/all_to_all | solution.py:71
  32.9 0.0 reduce-scatter.2.cloned.1.call-start
  33.0 0.5 broadcast.225
  33.5 0.7 reduce.24
  34.2 0.1 squeeze.31
  34.3 3.3 %all-to-all-done.1 = f32[8,1,144]{2,1,0:T(1,128)S(1)} async-done(((f32[8,1,144]{2,1,0:T(1,128)}), f32[8,1,144]{2,1,0:T(1,128)S(1)}, u32[]{:S(2)}, u32[]{:S(2)}) %all-to-all-start.1) | async-done | bytes 4640 | tf_op jit(solution)/shard_map/all_to_all | solution.py:71
  37.6 0.5 broadcast.232
  38.1 0.7 reduce.25
  38.8 0.1 reshape.198
  38.9 0.1 reshape.134
  39.0 3.4 %scatter_custom_fusion.2 = f32[131072]{0:T(1024)S(1)} fusion(s32[384]{0:T(512)S(1)} %fusion.95, f32[384]{0:T(512)S(1)} %reshape.134, f32[]{:T(128)} %constant.13.clone.1), kind=kCustom, calls=%fused_computation.160 | custom fusion | flops 384 | bytes 524292 | tf_op jit(solution)/shard_map/scatter-add | solution.py:82
  42.4 2.0 %select_maximum_fusion.4 = f32[12,264,136]{2,1,0:T(8,128)S(1)} fusion(f32[4,256,128]{2,1,0:T(8,128)S(1)} %collective-permute-done, f32[4,256,128]{2,1,0:T(8,128)} %bitcast.47, f32[4,256,128]{2,1,0:T(8,128)S(1)} %collective-permute-done.1), kind=kLoop, calls=%fused_computation.13 | loop fusion | flops 6462720 | bytes 3296256 | tf_op jit(solution)/shard_map/concatenate | solution.py:22
  44.4 3.2 %fusion.61 = f32[4,256,128]{2,1,0:T(8,128)S(1)} fusion(f32[4,256,128]{2,1,0:T(8,128)S(1)} %copy-done.1, f32[4,256,128]{2,1,0:T(8,128)S(1)} %bitcast.51, f32[4,256,128]{2,1,0:T(8,128)S(1)} %collective-permute-done.1, f32[4,256,128]{2,1,0:T(8,128)S(1)} %bitcast.48, f32[4,256,128]{2,1,0:T(8,128)S(1)} %collective-permute-done, ...), kind=kLoop, calls=%fused_computation.100 | loop fusion | flops 5242880 | bytes 12058624 | tf_op jit(solution)/shard_map/add | solution.py:88
  47.6 1.7 %collective-permute-start.3 = (f32[4,256,128]{2,1,0:T(8,128)S(1)}, f32[4,256,128]{2,1,0:T(8,128)S(1)}, u32[]{:S(2)}, u32[]{:S(2)}) collective-permute-start(f32[4,256,128]{2,1,0:T(8,128)S(1)} %fusion.61), channel_id=1, source_target_pairs={{0,1},{1,2},{2,3},{3,4},{4,5},{5,6},{6,7},{8,9},{9,10},{10,11},{11... | collective-permute-start | bytes 1572872 | tf_op jit(solution)/shard_map/ppermute | solution.py:18
  49.3 1.3 %collective-permute-start.2 = (f32[4,256,128]{2,1,0:T(8,128)S(1)}, f32[4,256,128]{2,1,0:T(8,128)S(1)}, u32[]{:S(2)}, u32[]{:S(2)}) collective-permute-start(f32[4,256,128]{2,1,0:T(8,128)S(1)} %fusion.61), channel_id=1, source_target_pairs={{1,0},{2,1},{3,2},{4,3},{5,4},{6,5},{7,6},{9,8},{10,9},{11,10},{12... | collective-permute-start | bytes 1572872 | tf_op jit(solution)/shard_map/ppermute | solution.py:21
  50.6 0.1 reshape.142
  50.7 4.1 %scatter_custom_fusion.3 = f32[131072]{0:T(1024)} fusion(s32[384]{0:T(512)S(1)} %fusion.95, f32[384]{0:T(512)S(1)} %reshape.142, f32[]{:T(128)} %constant.13.clone.1), kind=kCustom, calls=%fused_computation.158 | custom fusion | flops 384 | bytes 524292 | tf_op jit(solution)/shard_map/scatter-add | solution.py:82
  54.8 0.9 select_maximum_fusion.2
  55.7 3.2 %fusion.38 = f32[4,256,128]{2,1,0:T(8,128)S(1)} fusion(f32[4,256,128]{2,1,0:T(8,128)S(1)} %copy-done.1, f32[4,256,128]{2,1,0:T(8,128)} %bitcast.52, f32[4,256,128]{2,1,0:T(8,128)S(1)} %collective-permute-done.3, f32[4,256,128]{2,1,0:T(8,128)S(1)} %fusion.61, f32[4,256,128]{2,1,0:T(8,128)S(1)} %collective-permute-done.2, ...), kind=kLoop, calls=%fused_computation.77 | loop fusion | flops 5242880 | bytes 12058624 | tf_op jit(solution)/shard_map/add | solution.py:88
  58.9 0.0 copy-start.2
  58.9 10.7 %collective-permute-start.5 = (f32[4,256,128]{2,1,0:T(8,128)S(1)}, f32[4,256,128]{2,1,0:T(8,128)S(1)}, u32[]{:S(2)}, u32[]{:S(2)}) collective-permute-start(f32[4,256,128]{2,1,0:T(8,128)S(1)} %fusion.38), channel_id=1, source_target_pairs={{0,1},{1,2},{2,3},{3,4},{4,5},{5,6},{6,7},{8,9},{9,10},{10,11},{11... | collective-permute-start | bytes 1572872 | tf_op jit(solution)/shard_map/ppermute | solution.py:18
  69.6 1.5 %collective-permute-start.4 = (f32[4,256,128]{2,1,0:T(8,128)S(1)}, f32[4,256,128]{2,1,0:T(8,128)S(1)}, u32[]{:S(2)}, u32[]{:S(2)}) collective-permute-start(f32[4,256,128]{2,1,0:T(8,128)S(1)} %fusion.38), channel_id=1, source_target_pairs={{1,0},{2,1},{3,2},{4,3},{5,4},{6,5},{7,6},{9,8},{10,9},{11,10},{12... | collective-permute-start | bytes 1572872 | tf_op jit(solution)/shard_map/ppermute | solution.py:21
  71.1 0.1 reshape.150
  71.2 3.4 %scatter_custom_fusion.4 = f32[131072]{0:T(1024)S(1)} fusion(s32[384]{0:T(512)S(1)} %fusion.95, f32[384]{0:T(512)S(1)} %reshape.150, f32[]{:T(128)} %constant.13.clone.1), kind=kCustom, calls=%fused_computation.156 | custom fusion | flops 384 | bytes 524292 | tf_op jit(solution)/shard_map/scatter-add | solution.py:82
  74.6 0.0 copy-start.3
  74.6 0.9 select_maximum_fusion
  75.5 0.2 copy-done.3
  75.7 3.1 %fusion.81 = (f32[4,256,128]{2,1,0:T(8,128)}, f32[4,256,128]{2,1,0:T(8,128)}) fusion(f32[4,256,128]{2,1,0:T(8,128)S(1)} %fusion.38, f32[4,256,128]{2,1,0:T(8,128)S(1)} %fusion.61, bf16[1,3,4,256,128]{4,3,2,1,0:T(8,128)(2,1)S(1)} %copy-done.3, f32[4,256,128]{2,1,0:T(8,128)S(1)} %copy-done.1, f32[4,256,128]{2,1,0:T(8,128)S(1)} %bitcast.50, ...), kind=kLoop, calls=%fused_computation.151 | loop fusion | flops 6291456 | bytes 13369344 | tf_op jit(solution)/shard_map/add | solution.py:92
  78.8 0.0 reduce-scatter.2.cloned.1.call-update
  78.8 28.1 %reduce-scatter.2.cloned.1.call-done = f32[4,64,128]{2,1,0:T(8,128)} async-done(((f32[4,256,128]{2,1,0:T(8,128)}), f32[4,64,128]{2,1,0:T(8,128)}) %reduce-scatter.2.cloned.1.call-update) | async-done | bytes 131088 | tf_op jit(solution)/shard_map/reduce_scatter | solution.py:94
  (14 shorter events, 0.1 us)
Async XLA Ops:
  7.2 37.2 %copy-start = (f32[1,4,256,128]{3,2,1,0:T(8,128)S(1)}, f32[1,4,256,128]{3,2,1,0:T(8,128)}, u32[]{:S(2)}) copy-start(f32[1,4,256,128]{3,2,1,0:T(8,128)} %param.8) | copy-start | bytes 1572868
  7.2 37.2 %copy-start.1 = (f32[4,256,128]{2,1,0:T(8,128)S(1)}, f32[4,256,128]{2,1,0:T(8,128)}, u32[]{:S(2)}) copy-start(f32[4,256,128]{2,1,0:T(8,128)} %param.7) | copy-start | bytes 1572868
  7.2 35.2 %collective-permute-start.1 = (f32[4,256,128]{2,1,0:T(8,128)}, f32[4,256,128]{2,1,0:T(8,128)S(1)}, u32[]{:S(2)}, u32[]{:S(2)}) collective-permute-start(f32[4,256,128]{2,1,0:T(8,128)} %bitcast.45), channel_id=1, source_target_pairs={{0,1},{1,2},{2,3},{3,4},{4,5},{5,6},{6,7},{8,9},{9,10},{10,11},{11... | collective-permute-start | bytes 1572872 | tf_op jit(solution)/shard_map/ppermute | solution.py:18
  9.7 32.7 %collective-permute-start = (f32[4,256,128]{2,1,0:T(8,128)}, f32[4,256,128]{2,1,0:T(8,128)S(1)}, u32[]{:S(2)}, u32[]{:S(2)}) collective-permute-start(f32[4,256,128]{2,1,0:T(8,128)} %bitcast.46), channel_id=1, source_target_pairs={{1,0},{2,1},{3,2},{4,3},{5,4},{6,5},{7,6},{9,8},{10,9},{11,10},{12... | collective-permute-start | bytes 1572872 | tf_op jit(solution)/shard_map/ppermute | solution.py:21
  17.9 11.6 %all-to-all-start = ((s32[1,8,48]{2,0,1:T(1,128)}), s32[1,8,48]{2,0,1:T(1,128)S(1)}, u32[]{:S(2)}, u32[]{:S(2)}) async-start(s32[1,8,48]{2,0,1:T(1,128)} %all_to_all.12), calls=%async_computation | async-start | bytes 8192 | tf_op jit(solution)/shard_map/all_to_all | solution.py:72
  29.6 8.0 %all-to-all-start.1 = ((f32[8,1,144]{2,1,0:T(1,128)}), f32[8,1,144]{2,1,0:T(1,128)S(1)}, u32[]{:S(2)}, u32[]{:S(2)}) async-start(f32[8,1,144]{2,1,0:T(1,128)} %reshape.197), calls=%async_computation.1 | async-start | bytes 16384 | tf_op jit(solution)/shard_map/all_to_all | solution.py:71
  32.9 74.0 %reduce-scatter.2.cloned.1.call-start = ((), (), s32[]{:S(2)}) async-start(), calls=%async_computation.3 | async-start | bytes 655360 | tf_op jit(solution)/shard_map/reduce_scatter | solution.py:94
  47.6 7.2 %collective-permute-start.3 = (f32[4,256,128]{2,1,0:T(8,128)S(1)}, f32[4,256,128]{2,1,0:T(8,128)S(1)}, u32[]{:S(2)}, u32[]{:S(2)}) collective-permute-start(f32[4,256,128]{2,1,0:T(8,128)S(1)} %fusion.61), channel_id=1, source_target_pairs={{0,1},{1,2},{2,3},{3,4},{4,5},{5,6},{6,7},{8,9},{9,10},{10,11},{11... | collective-permute-start | bytes 1572872 | tf_op jit(solution)/shard_map/ppermute | solution.py:18
  49.3 5.4 %collective-permute-start.2 = (f32[4,256,128]{2,1,0:T(8,128)S(1)}, f32[4,256,128]{2,1,0:T(8,128)S(1)}, u32[]{:S(2)}, u32[]{:S(2)}) collective-permute-start(f32[4,256,128]{2,1,0:T(8,128)S(1)} %fusion.61), channel_id=1, source_target_pairs={{1,0},{2,1},{3,2},{4,3},{5,4},{6,5},{7,6},{9,8},{10,9},{11,10},{12... | collective-permute-start | bytes 1572872 | tf_op jit(solution)/shard_map/ppermute | solution.py:21
  58.9 19.9 %copy-start.2 = (f32[4,256,128]{2,1,0:T(8,128)}, f32[4,256,128]{2,1,0:T(8,128)S(1)}, u32[]{:S(2)}) copy-start(f32[4,256,128]{2,1,0:T(8,128)S(1)} %fusion.38) | copy-start | bytes 1572868
  58.9 15.7 %collective-permute-start.5 = (f32[4,256,128]{2,1,0:T(8,128)S(1)}, f32[4,256,128]{2,1,0:T(8,128)S(1)}, u32[]{:S(2)}, u32[]{:S(2)}) collective-permute-start(f32[4,256,128]{2,1,0:T(8,128)S(1)} %fusion.38), channel_id=1, source_target_pairs={{0,1},{1,2},{2,3},{3,4},{4,5},{5,6},{6,7},{8,9},{9,10},{10,11},{11... | collective-permute-start | bytes 1572872 | tf_op jit(solution)/shard_map/ppermute | solution.py:18
  69.6 5.0 %collective-permute-start.4 = (f32[4,256,128]{2,1,0:T(8,128)S(1)}, f32[4,256,128]{2,1,0:T(8,128)S(1)}, u32[]{:S(2)}, u32[]{:S(2)}) collective-permute-start(f32[4,256,128]{2,1,0:T(8,128)S(1)} %fusion.38), channel_id=1, source_target_pairs={{1,0},{2,1},{3,2},{4,3},{5,4},{6,5},{7,6},{9,8},{10,9},{11,10},{12... | collective-permute-start | bytes 1572872 | tf_op jit(solution)/shard_map/ppermute | solution.py:21
  74.6 1.1 copy-start.3
Sparse Core Ops, SparseCore 0:
  79.0 27.9 reduce-scatter.1
where the time goes:
time: 114 us
  waiting for transfers between devices  32.8 us (29%)
  starting transfers between devices  29.4 us (26%)
  other arithmetic  28.6 us (25%)
  between operations  14.3 us (13%)
  local copies, waits for them, and re-layouts  8.62 us (8%)
    reduce_scatter x1, waiting for transfers between devices, local(): lax.psum_scatter(image_acc, 'shot', scatter_dimension=1, tiled=True)  28.1 us
    ppermute x3, starting transfers between devices, with_halo(): lax.ppermute(lax.slice_in_dim(block, block.shape[dim] - width, None, axis...  14.9 us
    scatter-add x3, other arithmetic, local(): source = jnp.zeros((extent_x * extent_y * extent_z,), jnp.float32).at[her...  10.9 us
    all_to_all x1, starting transfers between devices, local(): lax.all_to_all(send_cells, 'space', split_axis=1, concat_axis=1, tiled=True)  7.05 us
    add x2, other arithmetic, local(): 2.0 * current - previous  6.43 us
    ppermute x3, starting transfers between devices, with_halo(): lax.ppermute(lax.slice_in_dim(block, 0, width, axis=dim), axis, backward)  4.06 us
    concatenate x3, other arithmetic, with_halo(): block = jnp.concatenate([low, block, high], axis=dim)  3.76 us
    all_to_all x1, starting transfers between devices, local(): lax.all_to_all(send_values, 'space', split_axis=1, concat_axis=1, tiled=T...  3.33 us
  transfers between devices with their start and end apart: 9, of which 3 were waited for; matrix products, arithmetic and copies ran while one was open for 20% of the time, Pallas kernels for 0%

commit v1 on v0

v1 whole, which is shorter than its diff:
```python
import functools

import jax
import jax.numpy as jnp
from jax import lax
from jax.experimental import pallas as pl
from jax.experimental.pallas import tpu as pltpu
from jax.sharding import PartitionSpec as P

CAP = 48
HALO = 4
PAD = 8
LANES = 128
PACK = 8
MESH = pl.DeviceIdType.MESH
STENCIL_WEIGHTS = (-205.0 / 72.0, 8.0 / 5.0, -1.0 / 5.0, 8.0 / 315.0, -1.0 / 560.0)


def kernel(
    slabs, shots, steps, extent, block_rows,
    slab_ref, cell_ref, res_ref, now_hbm, old_hbm, cour_hbm, fwd_hbm,
    last_hbm, prior_hbm, image_ref,
    ext, old_v, cour_v, fwd_v, last_v, src_v, data_v, pack_v, got_v, img_send, img_recv,
    load_sem, out_sem, halo_send, halo_recv, rec_send, rec_recv, img_ssem, img_rsem,
):
    cx, ny, nz = extent
    rows = ny // shots
    me = lax.axis_index("space")
    shot = lax.axis_index("shot")

    load_now = pltpu.make_async_copy(
        now_hbm.at[0], ext.at[0, pl.ds(HALO, cx), pl.ds(PAD, ny)], load_sem.at[0]
    )
    load_old = pltpu.make_async_copy(old_hbm.at[0], old_v, load_sem.at[1])
    load_cour = pltpu.make_async_copy(cour_hbm, cour_v, load_sem.at[2])
    load_fwd = pltpu.make_async_copy(fwd_hbm.at[0], fwd_v, load_sem.at[3])
    for copy in (load_now, load_old, load_cour, load_fwd):
        copy.start()

    barrier = pltpu.get_barrier_semaphore()
    for delta in range(1, slabs):
        pl.semaphore_signal(
            barrier, inc=1, device_id=(shot, lax.rem(me + delta, slabs)), device_id_type=MESH
        )
    for delta in range(1, shots):
        pl.semaphore_signal(
            barrier, inc=1, device_id=(lax.rem(shot + delta, shots), me), device_id_type=MESH
        )
    pl.semaphore_wait(barrier, slabs - 1 + shots - 1)

    def first_row(i):
        return pl.multiple_of(lax.rem(shot + 1 + i, shots) * rows, rows)

    def halo_copy(step, i, side):
        at = first_row(i)
        if step == 0:
            source = now_hbm.at[0, :, pl.ds(at, rows)]
        else:
            source = ext.at[step, pl.ds(HALO, cx), pl.ds(at + PAD, rows)]
        low_at = HALO + cx if side == 0 else 0
        return pltpu.make_async_remote_copy(
            src_ref=source,
            dst_ref=ext.at[step, pl.ds(low_at, HALO), pl.ds(at + PAD, rows)],
            send_sem=halo_send.at[step, side, i],
            recv_sem=halo_recv.at[step, side, i],
            device_id=(shot, me - 1 if side == 0 else me + 1),
            device_id_type=MESH,
        )

    has_low, has_high = me > 0, me < slabs - 1

    def send_halo(step, i):
        @pl.when(has_low)
        def _():
            halo_copy(step, i, 0).start()

        @pl.when(has_high)
        def _():
            halo_copy(step, i, 1).start()

    def wait_halo(step, i):
        @pl.when(has_high)
        def _():
            halo_copy(step, i, 0).wait_recv()

        @pl.when(has_low)
        def _():
            halo_copy(step, i, 1).wait_recv()

    def wait_sent(step, i):
        @pl.when(has_low)
        def _():
            halo_copy(step, i, 0).wait_send()

        @pl.when(has_high)
        def _():
            halo_copy(step, i, 1).wait_send()

    def loop(count, body):
        lax.fori_loop(0, count, lambda i, c: (body(i), c)[1], 0)

    count = slab_ref.shape[1]
    row = slab_ref[...]
    cells = cell_ref[...]
    first = lax.broadcasted_iota(jnp.int32, (count, count), 0)
    second = lax.broadcasted_iota(jnp.int32, (count, count), 1)
    column = jnp.sum(jnp.where(first == second, row, 0), axis=1, keepdims=True)
    earlier = jnp.where((column == row) & (first < second), 1, 0)
    rank = jnp.sum(earlier, axis=0, keepdims=True)
    lane = rank + lax.rem(me, 2) * CAP
    data_v[...] = jnp.zeros_like(data_v)
    data_v[0:steps] = res_ref[0]
    data_v[steps : steps + 1] = lax.div(cells, nz).astype(jnp.float32)
    data_v[steps + 1 : steps + 2] = lax.rem(cells, nz).astype(jnp.float32)
    slots = lax.broadcasted_iota(jnp.int32, (LANES, count), 0)

    def pack(d):
        onehot = jnp.where((slots == lane) & (row == d), 1.0, 0.0)
        pack_v[d] = lax.dot_general(
            data_v[...], onehot, (((1,), (1,)), ((), ())),
            precision=lax.Precision.HIGHEST, preferred_element_type=jnp.float32,
        )

    def rec_copy(delta):
        to = lax.rem(me + delta, slabs)
        return pltpu.make_async_remote_copy(
            src_ref=pack_v.at[to], dst_ref=got_v.at[me],
            send_sem=rec_send.at[to], recv_sem=rec_recv.at[me],
            device_id=(shot, to), device_id_type=MESH,
        )

    def rec_arrival(delta):
        source = lax.rem(me + delta, slabs)
        return pltpu.make_async_remote_copy(
            src_ref=pack_v.at[source], dst_ref=got_v.at[source],
            send_sem=rec_send.at[source], recv_sem=rec_recv.at[source],
            device_id=(shot, source), device_id_type=MESH,
        )

    send_halo(0, 0)
    loop(slabs, pack)
    for delta in range(1, slabs):
        rec_copy(delta).start()
    loop(shots - 1, lambda i: send_halo(0, i + 1))
    got_v[me] = pack_v[me]

    edge = jnp.zeros((cx, PAD, nz), jnp.float32)
    for step in range(steps):
        ext[step, HALO : HALO + cx, 0:PAD] = edge
        ext[step, HALO : HALO + cx, PAD + ny :] = edge

    def clear(low_at):
        for step in range(steps):
            for layer in range(HALO):
                ext[step, low_at + layer] = jnp.zeros((ny + 2 * PAD, nz), jnp.float32)

    @pl.when(me == 0)
    def _():
        clear(0)

    @pl.when(me == slabs - 1)
    def _():
        clear(HALO + cx)

    for delta in range(1, slabs):
        rec_arrival(delta).wait_recv()
    flat = cx * ny
    group = 4
    for step in range(steps):
        src_v[step] = jnp.zeros((flat, nz), jnp.float32)

    def add_sources(g):
        held = jnp.concatenate(
            [got_v[g * group] + got_v[g * group + 1], got_v[g * group + 2] + got_v[g * group + 3]], axis=1
        )
        where_row = held[steps : steps + 1].astype(jnp.int32)
        where_lane = held[steps + 1 : steps + 2].astype(jnp.int32)
        width = held.shape[1]
        picks = jnp.where(
            lax.broadcasted_iota(jnp.int32, (flat, width), 0) == where_row, 1.0, 0.0
        ).astype(jnp.bfloat16)
        hits = lax.broadcasted_iota(jnp.int32, (nz, width), 0) == where_lane
        for step in range(steps):
            rest = jnp.where(hits, held[step : step + 1], 0.0)
            total = None
            for _ in range(3):
                piece = rest.astype(jnp.bfloat16)
                rest = rest - piece.astype(jnp.float32)
                term = lax.dot_general(
                    picks, piece, (((1,), (1,)), ((), ())), preferred_element_type=jnp.float32
                )
                total = term if total is None else total + term
            src_v[step] += total

    loop(slabs // group, add_sources)
    for copy in (load_now, load_old, load_cour, load_fwd):
        copy.wait()

    def img_copy(i):
        return pltpu.make_async_remote_copy(
            src_ref=img_send.at[i], dst_ref=img_recv.at[i],
            send_sem=img_ssem.at[i], recv_sem=img_rsem.at[i],
            device_id=(lax.rem(shot + 1 + i, shots), me), device_id_type=MESH,
        )

    def out_copy(which, i):
        at = first_row(i)
        if which == 0:
            return pltpu.make_async_copy(
                last_v.at[:, pl.ds(at, rows)], last_hbm.at[0, :, pl.ds(at, rows)], out_sem.at[0, i]
            )
        return pltpu.make_async_copy(
            ext.at[steps - 1, pl.ds(HALO, cx), pl.ds(at + PAD, rows)],
            prior_hbm.at[0, :, pl.ds(at, rows)], out_sem.at[1, i],
        )

    z_at = lax.broadcasted_iota(jnp.int32, (block_rows, nz), 1)

    def update(step, i):
        start = first_row(i)

        def block(b):
            at = pl.multiple_of(start + b * block_rows, block_rows)
            for x in range(cx):
                center = ext[step, HALO + x, pl.ds(at + PAD, block_rows), :]
                summed = (3.0 * STENCIL_WEIGHTS[0]) * center
                for k in range(1, 5):
                    along = ext[step, HALO + x + k, pl.ds(at + PAD, block_rows), :]
                    along += ext[step, HALO + x - k, pl.ds(at + PAD, block_rows), :]
                    along += ext[step, HALO + x, pl.ds(at + PAD + k, block_rows), :]
                    along += ext[step, HALO + x, pl.ds(at + PAD - k, block_rows), :]
                    along += jnp.where(z_at < nz - k, pltpu.roll(center, nz - k, 1), 0.0)
                    along += jnp.where(z_at >= k, pltpu.roll(center, k, 1), 0.0)
                    summed += STENCIL_WEIGHTS[k] * along
                if step == 0:
                    before = old_v[x, pl.ds(at, block_rows), :]
                else:
                    before = ext[step - 1, HALO + x, pl.ds(at + PAD, block_rows), :]
                source = src_v[step, pl.ds(pl.multiple_of(x * ny + at, block_rows), block_rows), :]
                speed = cour_v[x, pl.ds(at, block_rows), :]
                fresh = 2.0 * center - before + speed * (summed + source)
                if step < steps - 1:
                    ext[step + 1, HALO + x, pl.ds(at + PAD, block_rows), :] = fresh
                else:
                    last_v[x, pl.ds(at, block_rows), :] = fresh
                    image = fwd_v[steps - 1, x, pl.ds(at, block_rows), :].astype(jnp.float32) * fresh
                    for s in range(steps - 1):
                        field = ext[s + 1, HALO + x, pl.ds(at + PAD, block_rows), :]
                        image += fwd_v[s, x, pl.ds(at, block_rows), :].astype(jnp.float32) * field
                    img_send[i, x, pl.ds(pl.multiple_of(b * block_rows, block_rows), block_rows), :] = image

        loop(rows // block_rows, block)

    for step in range(steps):

        def chunk(i, step=step):
            wait_halo(step, i)
            update(step, i)
            if step < steps - 1:
                send_halo(step + 1, i)
            if step == steps - 2:
                out_copy(1, i).start()
            if step == steps - 1:
                out_copy(0, i).start()

                @pl.when(i < shots - 1)
                def _():
                    img_copy(i).start()

        loop(shots, chunk)

    for i in range(shots - 1):
        img_copy(i).wait_recv()
    for x in range(cx):
        total = img_send[shots - 1, x]
        for i in range(shots - 1):
            total += img_recv[i, x]
        image_ref[x] = total

    for step in range(steps):
        loop(shots, lambda i, step=step: wait_sent(step, i))
    for delta in range(1, slabs):
        rec_copy(delta).wait_send()
    for i in range(shots - 1):
        img_copy(i).wait_send()
    loop(shots, lambda i: (out_copy(0, i).wait(), out_copy(1, i).wait()))


def solution(mesh):
    slabs, shots = mesh.shape["space"], mesh.shape["shot"]

    def local(courant, now, old, receiver_slab, receiver_cell, residuals, forward):
        cx, ny, nz = courant.shape
        steps = residuals.shape[1]
        rows = ny // shots
        block_rows = min(16, rows)
        anywhere = pl.BlockSpec(memory_space=pl.ANY)
        vmem = pl.BlockSpec(memory_space=pltpu.VMEM)
        f32 = jnp.float32
        dma = pltpu.SemaphoreType.DMA
        return pl.pallas_call(
            functools.partial(kernel, slabs, shots, steps, (cx, ny, nz), block_rows),
            out_shape=(
                jax.ShapeDtypeStruct(now.shape, f32),
                jax.ShapeDtypeStruct(now.shape, f32),
                jax.ShapeDtypeStruct((cx, rows, nz), f32),
            ),
            in_specs=[vmem] * 3 + [anywhere] * 4,
            out_specs=(anywhere, anywhere, vmem),
            scratch_shapes=[
                pltpu.VMEM((steps, cx + 2 * HALO, ny + 2 * PAD, nz), f32),
                pltpu.VMEM((cx, ny, nz), f32),
                pltpu.VMEM((cx, ny, nz), f32),
                pltpu.VMEM(forward.shape[1:], forward.dtype),
                pltpu.VMEM((cx, ny, nz), f32),
                pltpu.VMEM((steps, cx * ny, nz), f32),
                pltpu.VMEM((PACK, receiver_cell.shape[1]), f32),
                pltpu.VMEM((slabs, PACK, LANES), f32),
                pltpu.VMEM((slabs, PACK, LANES), f32),
                pltpu.VMEM((shots, cx, rows, nz), f32),
                pltpu.VMEM((shots, cx, rows, nz), f32),
                dma((4,)),
                dma((2, shots)),
                dma((steps, 2, shots)),
                dma((steps, 2, shots)),
                dma((slabs,)),
                dma((slabs,)),
                dma((shots,)),
                dma((shots,)),
            ],
            compiler_params=pltpu.CompilerParams(
                collective_id=0, has_side_effects=True, vmem_limit_bytes=48 * 1024 * 1024
            ),
        )(receiver_slab.reshape(receiver_cell.shape), receiver_cell, residuals, now, old, courant, forward)

    in_specs = (
        P("space", None, None),
        P("shot", "space", None, None),
        P("shot", "space", None, None),
        P("shot", "space", None),
        P("shot", "space"),
        P("shot", None, "space"),
        P("shot", None, "space", None, None),
    )
    out_specs = (
        P("shot", "space", None, None),
        P("shot", "space", None, None),
        P("space", "shot", None),
    )
    return jax.shard_map(local, mesh=mesh, in_specs=in_specs, out_specs=out_specs, check_vma=False)
```

time: 114 us -> 51.3 us (0.45)
  the two profiles are of different devices: /device:TPU:0 before, /device:TPU:1 now
where the time goes in v1:
time: 51.3 us; the launch traced here: 51 us
  Pallas kernels  43.1 us (84%)
  local copies, waits for them, and re-layouts  7.21 us (14%)
  between operations  0.66 us (1%)
    pallas_call x1, Pallas kernels, local(): pl.pallas_call(functools.partial(kernel, slabs, shots, steps, (cx, ny, nz...  43.1 us
    unnamed x16, local copies, waits for them, and re-layouts  7.21 us

profile of v1, /device:TPU:1, one launch (start us, length us, event | category | flops | bytes accessed | tf_op | source)
XLA Modules:
  0.0 51.0 jit_solution(33133606857316471)
XLA Ops:
  0.6 0.0 copy-start.4
  0.6 0.0 copy-start.5
  0.7 0.7 %copy.10.res_ref = f32[1,3,384]{2,1,0:T(4,128)S(1)} copy(f32[1,3,384]{2,0,1:T(1,128)} %param.12) | data formatting | bytes 9216 | tf_op args[5]
  1.4 0.0 copy-done.4
  1.4 0.0 copy-done.5
  1.4 0.0 copy-start
  1.4 1.1 %copy-done = bf16[1,3,4,256,128]{4,3,2,1,0:T(8,128)(2,1)S(1)} copy-done((bf16[1,3,4,256,128]{4,3,2,1,0:T(8,128)(2,1)S(1)}, bf16[1,3,4,256,128]{4,3,2,1,0:T(8,128)(2,1)}, u32[]{:S(2)}) %copy-start) | copy-done | bytes 786456
  2.5 0.0 copy-start.1
  2.5 1.0 %copy-done.1 = f32[1,4,256,128]{3,2,1,0:T(8,128)S(1)} copy-done((f32[1,4,256,128]{3,2,1,0:T(8,128)S(1)}, f32[1,4,256,128]{3,2,1,0:T(8,128)}, u32[]{:S(2)}) %copy-start.1) | copy-done | bytes 524312
  3.5 0.0 copy-start.2
  3.5 1.0 %copy-done.2 = f32[1,4,256,128]{3,2,1,0:T(8,128)S(1)} copy-done((f32[1,4,256,128]{3,2,1,0:T(8,128)S(1)}, f32[1,4,256,128]{3,2,1,0:T(8,128)}, u32[]{:S(2)}) %copy-start.2) | copy-done | bytes 524312
  4.6 0.0 copy-start.3
  4.6 1.0 %copy-done.3 = f32[4,256,128]{2,1,0:T(8,128)S(1)} copy-done((f32[4,256,128]{2,1,0:T(8,128)S(1)}, f32[4,256,128]{2,1,0:T(8,128)}, u32[]{:S(2)}) %copy-start.3) | copy-done | bytes 524312
  5.6 43.1 %shard_map.94 = (f32[1,4,256,128]{3,2,1,0:T(8,128)S(1)}, f32[1,4,256,128]{3,2,1,0:T(8,128)S(1)}, f32[4,64,128]{2,1,0:T(8,128)S(1)}) custom-call(s32[1,384]{1,0:T(1,128)S(1)} %bitcast.1, s32[1,384]{1,0:T(1,128)S(1)} %copy-done.5, f32[1,3,384]{2,1,0:T(4,128)S(1)} %copy.10.res_ref, f32[1,4,256,128]{3,2,1,0:T(8,128)S(1)} %copy-done.1, ...), custom_call_target="tpu_custom_call" | custom-call | tf_op jit(solution)/shard_map/pallas_call | solution.py:301
  48.7 0.8 %copy.14 = f32[1,4,256,128]{3,2,1,0:T(8,128)} copy(f32[1,4,256,128]{3,2,1,0:T(8,128)S(1)} %get-tuple-element.6) | data formatting | bytes 1048576
  49.5 0.8 %copy.15 = f32[1,4,256,128]{3,2,1,0:T(8,128)} copy(f32[1,4,256,128]{3,2,1,0:T(8,128)S(1)} %get-tuple-element.7) | data formatting | bytes 1048576
  50.3 0.7 %copy.16 = f32[4,64,128]{2,1,0:T(8,128)} copy(f32[4,64,128]{2,1,0:T(8,128)S(1)} %get-tuple-element.8) | data formatting | bytes 262144
Async XLA Ops:
  0.6 0.7 %copy-start.4 = (s32[1,384,1]{1,2,0:T(1,128)S(1)}, s32[1,384,1]{1,2,0:T(1,128)}, u32[]{:S(2)}) copy-start(s32[1,384,1]{1,2,0:T(1,128)} %param.10) | copy-start | bytes 4612
  0.6 0.7 %copy-start.5 = (s32[1,384]{1,0:T(1,128)S(1)}, s32[1,384]{1,0:T(1,128)}, u32[]{:S(2)}) copy-start(s32[1,384]{1,0:T(1,128)} %cell_ref.1) | copy-start | bytes 4612
  1.4 1.1 %copy-start = (bf16[1,3,4,256,128]{4,3,2,1,0:T(8,128)(2,1)S(1)}, bf16[1,3,4,256,128]{4,3,2,1,0:T(8,128)(2,1)}, u32[]{:S(2)}) copy-start(bf16[1,3,4,256,128]{4,3,2,1,0:T(8,128)(2,1)} %fwd_hbm.1) | copy-start | bytes 2359300
  2.5 1.0 %copy-start.1 = (f32[1,4,256,128]{3,2,1,0:T(8,128)S(1)}, f32[1,4,256,128]{3,2,1,0:T(8,128)}, u32[]{:S(2)}) copy-start(f32[1,4,256,128]{3,2,1,0:T(8,128)} %now_hbm.1) | copy-start | bytes 1572868
  3.5 1.0 %copy-start.2 = (f32[1,4,256,128]{3,2,1,0:T(8,128)S(1)}, f32[1,4,256,128]{3,2,1,0:T(8,128)}, u32[]{:S(2)}) copy-start(f32[1,4,256,128]{3,2,1,0:T(8,128)} %old_hbm.1) | copy-start | bytes 1572868
  4.6 1.0 %copy-start.3 = (f32[4,256,128]{2,1,0:T(8,128)S(1)}, f32[4,256,128]{2,1,0:T(8,128)}, u32[]{:S(2)}) copy-start(f32[4,256,128]{2,1,0:T(8,128)} %cour_hbm.1) | copy-start | bytes 1572868

commit v2 on v1

--- a/solution.py
+++ b/solution.py
@@ -11,6 +11,7 @@
 HALO = 4
 PAD = 8
 LANES = 128
+VMEM_BYTES = 62 * 1024 * 1024
 PACK = 8
 MESH = pl.DeviceIdType.MESH
 STENCIL_WEIGHTS = (-205.0 / 72.0, 8.0 / 5.0, -1.0 / 5.0, 8.0 / 315.0, -1.0 / 560.0)
@@ -18,10 +19,11 @@
 
 def kernel(
     slabs, shots, steps, extent, block_rows,
-    slab_ref, cell_ref, res_ref, now_hbm, old_hbm, cour_hbm, fwd_hbm,
-    last_hbm, prior_hbm, image_ref,
-    ext, old_v, cour_v, fwd_v, last_v, src_v, data_v, pack_v, got_v, img_send, img_recv,
+    slab_hbm, cell_hbm, res_hbm, now_hbm, old_hbm, cour_hbm, fwd_hbm,
+    last_hbm, prior_hbm, image_hbm,
+    slab_ref, cell_ref, res_ref, ext, old_v, cour_v, fwd_v, last_v, src_v, data_v, pack_v, got_v, img_send, img_recv, image_ref, relay_v,
     load_sem, out_sem, halo_send, halo_recv, rec_send, rec_recv, img_ssem, img_rsem,
+    diag_send, diag_recv, relay_send, relay_recv,
 ):
     cx, ny, nz = extent
     rows = ny // shots
@@ -34,7 +36,13 @@
     load_old = pltpu.make_async_copy(old_hbm.at[0], old_v, load_sem.at[1])
     load_cour = pltpu.make_async_copy(cour_hbm, cour_v, load_sem.at[2])
     load_fwd = pltpu.make_async_copy(fwd_hbm.at[0], fwd_v, load_sem.at[3])
-    for copy in (load_now, load_old, load_cour, load_fwd):
+    small_loads = [
+        pltpu.make_async_copy(source, target, load_sem.at[4 + at])
+        for at, (source, target) in enumerate(
+            ((slab_hbm, slab_ref), (cell_hbm, cell_ref), (res_hbm, res_ref))
+        )
+    ]
+    for copy in (*small_loads, load_now, load_old, load_cour, load_fwd):
         copy.start()
 
     barrier = pltpu.get_barrier_semaphore()
@@ -67,38 +75,139 @@
             device_id_type=MESH,
         )
 
+    quad = slabs % 4 == 0 and cx % 2 == 0
+    half = cx // 2
+    turn = lax.rem(me, 4)
     has_low, has_high = me > 0, me < slabs - 1
+    if quad:
+        diag_low, diag_high = has_low & (turn == 0), has_high & (turn == 3)
+        near_low, near_high = has_low & (turn != 0), has_high & (turn != 3)
+        relay_lower, relay_upper = (turn == 0) & (me + 4 < slabs), (turn == 3) & (me >= 7)
+    else:
+        near_low, near_high = has_low, has_high
+
+    def diag_copy(step, i, up, h):
+        at = first_row(i)
+        if step == 0:
+            source = now_hbm.at[0, pl.ds(h * half, half), pl.ds(at, rows)]
+        else:
+            source = ext.at[step, pl.ds(HALO + h * half, half), pl.ds(at + PAD, rows)]
+        lower = me - 3 if up else me - 4
+        return pltpu.make_async_remote_copy(
+            src_ref=source,
+            dst_ref=relay_v.at[step * shots + i, 0 if up else 1],
+            send_sem=diag_send.at[step, h, i],
+            recv_sem=relay_recv.at[step * shots + i, 0 if up else 1],
+            device_id=(shot, lower + 7 * h),
+            device_id_type=MESH,
+        )
+
+    def relay_copy(g, up, h):
+        step, i = lax.div(g, shots), lax.rem(g, shots)
+        low_at = (0 if up else HALO + cx) + h * half
+        to = (me + 4 if up else me + 3) - 7 * h
+        return pltpu.make_async_remote_copy(
+            src_ref=relay_v.at[g, 0 if up else 1],
+            dst_ref=ext.at[step, pl.ds(low_at, half), pl.ds(first_row(i) + PAD, rows)],
+            send_sem=relay_send.at[g, 0 if up else 1],
+            recv_sem=diag_recv.at[step, h, i],
+            device_id=(shot, to),
+            device_id_type=MESH,
+        )
+
+    def relay_arrival(g, up):
+        slot = relay_v.at[g, 0 if up else 1]
+        return pltpu.make_async_remote_copy(
+            src_ref=slot, dst_ref=slot,
+            send_sem=relay_send.at[g, 0 if up else 1],
+            recv_sem=relay_recv.at[g, 0 if up else 1],
+            device_id=(shot, me), device_id_type=MESH,
+        )
+
+    def forward(g):
+        if quad:
+            for h, here in ((0, relay_lower), (1, relay_upper)):
+
+                @pl.when(here)
+                def _(h=h):
+                    for up in (True, False):
+                        relay_arrival(g, up).wait_recv()
+                        relay_copy(g, up, h).start()
+
+    def forwarded(g):
+        if quad:
+            for h, here in ((0, relay_lower), (1, relay_upper)):
+
+                @pl.when(here)
+                def _(h=h):
+                    for up in (True, False):
+                        relay_copy(g, up, h).wait_send()
 
     def send_halo(step, i):
-        @pl.when(has_low)
+        if quad:
+            for up, here in ((False, diag_low), (True, diag_high)):
+
+                @pl.when(here)
+                def _(up=up):
+                    for h in range(2):
+                        diag_copy(step, i, up, h).start()
+
+        @pl.when(near_low)
         def _():
             halo_copy(step, i, 0).start()
 
-        @pl.when(has_high)
+        @pl.when(near_high)
         def _():
             halo_copy(step, i, 1).start()
 
     def wait_halo(step, i):
-        @pl.when(has_high)
+        @pl.when(near_high)
         def _():
             halo_copy(step, i, 0).wait_recv()
 
-        @pl.when(has_low)
+        @pl.when(near_low)
         def _():
             halo_copy(step, i, 1).wait_recv()
 
+        if quad:
+            for up, here in ((True, diag_low), (False, diag_high)):
+
+                @pl.when(here)
+                def _(up=up):
+                    for h in range(2):
+                        low_at = (0 if up else HALO + cx) + h * half
+                        slot = ext.at[step, pl.ds(low_at, half), pl.ds(first_row(i) + PAD, rows)]
+                        pltpu.make_async_remote_copy(
+                            src_ref=slot, dst_ref=slot,
+                            send_sem=diag_send.at[step, h, i],
+                            recv_sem=diag_recv.at[step, h, i],
+                            device_id=(shot, me), device_id_type=MESH,
+                        ).wait_recv()
+
     def wait_sent(step, i):
-        @pl.when(has_low)
+        if quad:
+            for up, here in ((False, diag_low), (True, diag_high)):
+
+                @pl.when(here)
+                def _(up=up):
+                    for h in range(2):
+                        diag_copy(step, i, up, h).wait_send()
+
+        @pl.when(near_low)
         def _():
             halo_copy(step, i, 0).wait_send()
 
-        @pl.when(has_high)
+        @pl.when(near_high)
         def _():
             halo_copy(step, i, 1).wait_send()
 
     def loop(count, body):
         lax.fori_loop(0, count, lambda i, c: (body(i), c)[1], 0)
 
+    send_halo(0, 0)
+
+    for copy in small_loads:
+        copy.wait()
     count = slab_ref.shape[1]
     row = slab_ref[...]
     cells = cell_ref[...]
@@ -109,7 +218,8 @@
     rank = jnp.sum(earlier, axis=0, keepdims=True)
     lane = rank + lax.rem(me, 2) * CAP
     data_v[...] = jnp.zeros_like(data_v)
-    data_v[0:steps] = res_ref[0]
+    for step in range(steps):
+        data_v[step : step + 1] = res_ref[step]
     data_v[steps : steps + 1] = lax.div(cells, nz).astype(jnp.float32)
     data_v[steps + 1 : steps + 2] = lax.rem(cells, nz).astype(jnp.float32)
     slots = lax.broadcasted_iota(jnp.int32, (LANES, count), 0)
@@ -137,7 +247,6 @@
             device_id=(shot, source), device_id_type=MESH,
         )
 
-    send_halo(0, 0)
     loop(slabs, pack)
     for delta in range(1, slabs):
         rec_copy(delta).start()
@@ -162,16 +271,19 @@
     def _():
         clear(HALO + cx)
 
+    lead = shots // 2
+    forward(0)
+
     for delta in range(1, slabs):
         rec_arrival(delta).wait_recv()
     flat = cx * ny
-    group = 4
+    group = 8 if slabs % 8 == 0 else 2
     for step in range(steps):
         src_v[step] = jnp.zeros((flat, nz), jnp.float32)
 
     def add_sources(g):
         held = jnp.concatenate(
-            [got_v[g * group] + got_v[g * group + 1], got_v[g * group + 2] + got_v[g * group + 3]], axis=1
+            [got_v[g * group + 2 * p] + got_v[g * group + 2 * p + 1] for p in range(group // 2)], axis=1
         )
         where_row = held[steps : steps + 1].astype(jnp.int32)
         where_lane = held[steps + 1 : steps + 2].astype(jnp.int32)
@@ -180,19 +292,23 @@
             lax.broadcasted_iota(jnp.int32, (flat, width), 0) == where_row, 1.0, 0.0
         ).astype(jnp.bfloat16)
         hits = lax.broadcasted_iota(jnp.int32, (nz, width), 0) == where_lane
+        rest = jnp.concatenate(
+            [jnp.where(hits, held[step : step + 1], 0.0) for step in range(steps)], axis=0
+        )
+        total = None
+        for _ in range(3):
+            piece = rest.astype(jnp.bfloat16)
+            rest = rest - piece.astype(jnp.float32)
+            term = lax.dot_general(
+                picks, piece, (((1,), (1,)), ((), ())), preferred_element_type=jnp.float32
+            )
+            total = term if total is None else total + term
         for step in range(steps):
-            rest = jnp.where(hits, held[step : step + 1], 0.0)
-            total = None
-            for _ in range(3):
-                piece = rest.astype(jnp.bfloat16)
-                rest = rest - piece.astype(jnp.float32)
-                term = lax.dot_general(
-                    picks, piece, (((1,), (1,)), ((), ())), preferred_element_type=jnp.float32
-                )
-                total = term if total is None else total + term
-            src_v[step] += total
+            src_v[step] += total[:, step * nz : (step + 1) * nz]
 
     loop(slabs // group, add_sources)
+    for g in range(1, lead):
+        forward(g)
     for copy in (load_now, load_old, load_cour, load_fwd):
         copy.wait()
 
@@ -254,6 +370,12 @@
     for step in range(steps):
 
         def chunk(i, step=step):
+            ahead = step * shots + i + lead
+
+            @pl.when(ahead < steps * shots)
+            def _():
+                forward(ahead)
+
             wait_halo(step, i)
             update(step, i)
             if step < steps - 1:
@@ -276,6 +398,8 @@
         for i in range(shots - 1):
             total += img_recv[i, x]
         image_ref[x] = total
+    image_out = pltpu.make_async_copy(image_ref, image_hbm, load_sem.at[7])
+    image_out.start()
 
     for step in range(steps):
         loop(shots, lambda i, step=step: wait_sent(step, i))
@@ -283,7 +407,22 @@
         rec_copy(delta).wait_send()
     for i in range(shots - 1):
         img_copy(i).wait_send()
+    loop(steps * shots, forwarded)
+    image_out.wait()
     loop(shots, lambda i: (out_copy(0, i).wait(), out_copy(1, i).wait()))
+
+
+def store(*refs):
+    count = len(refs) // 3
+    copies = []
+    for at in range(count):
+        source, target, sems = refs[at], refs[count + at], refs[2 * count + at]
+        for part in range(sems.shape[0]):
+            copies.append(pltpu.make_async_copy(source.at[part], target.at[part], sems.at[part]))
+    for copy in copies:
+        copy.start()
+    for copy in copies:
+        copy.wait()
 
 
 def solution(mesh):
@@ -295,19 +434,22 @@
         rows = ny // shots
         block_rows = min(16, rows)
         anywhere = pl.BlockSpec(memory_space=pl.ANY)
-        vmem = pl.BlockSpec(memory_space=pltpu.VMEM)
         f32 = jnp.float32
         dma = pltpu.SemaphoreType.DMA
-        return pl.pallas_call(
+        hbm = pl.BlockSpec(memory_space=pltpu.HBM)
+        parts = pl.pallas_call(
             functools.partial(kernel, slabs, shots, steps, (cx, ny, nz), block_rows),
             out_shape=(
-                jax.ShapeDtypeStruct(now.shape, f32),
-                jax.ShapeDtypeStruct(now.shape, f32),
+                jax.ShapeDtypeStruct((1, cx, ny, nz), f32),
+                jax.ShapeDtypeStruct((1, cx, ny, nz), f32),
                 jax.ShapeDtypeStruct((cx, rows, nz), f32),
             ),
-            in_specs=[vmem] * 3 + [anywhere] * 4,
-            out_specs=(anywhere, anywhere, vmem),
+            in_specs=[hbm] * 7,
+            out_specs=(anywhere,) * 3,
             scratch_shapes=[
+                pltpu.VMEM(receiver_cell.shape, jnp.int32),
+                pltpu.VMEM(receiver_cell.shape, jnp.int32),
+                pltpu.VMEM((steps, 1, receiver_cell.shape[1]), f32),
                 pltpu.VMEM((steps, cx + 2 * HALO, ny + 2 * PAD, nz), f32),
                 pltpu.VMEM((cx, ny, nz), f32),
                 pltpu.VMEM((cx, ny, nz), f32),
@@ -319,7 +461,9 @@
                 pltpu.VMEM((slabs, PACK, LANES), f32),
                 pltpu.VMEM((shots, cx, rows, nz), f32),
                 pltpu.VMEM((shots, cx, rows, nz), f32),
-                dma((4,)),
+                pltpu.VMEM((cx, rows, nz), f32),
+                pltpu.VMEM((steps * shots, 2, cx // 2, rows, nz), f32),
+                dma((8,)),
                 dma((2, shots)),
                 dma((steps, 2, shots)),
                 dma((steps, 2, shots)),
@@ -327,11 +471,28 @@
                 dma((slabs,)),
                 dma((shots,)),
                 dma((shots,)),
+                dma((steps, 2, shots)),
+                dma((steps, 2, shots)),
+                dma((steps * shots, 2)),
+                dma((steps * shots, 2)),
             ],
             compiler_params=pltpu.CompilerParams(
-                collective_id=0, has_side_effects=True, vmem_limit_bytes=48 * 1024 * 1024
+                collective_id=0, has_side_effects=True, vmem_limit_bytes=VMEM_BYTES
             ),
-        )(receiver_slab.reshape(receiver_cell.shape), receiver_cell, residuals, now, old, courant, forward)
+        )(
+            receiver_slab.reshape(receiver_cell.shape), receiver_cell,
+            jnp.transpose(residuals, (1, 0, 2)), now, old, courant, forward,
+        )
+        last, prior = (part.reshape(cx, ny, nz) for part in parts[:2])
+        last, prior, image = pl.pallas_call(
+            store,
+            out_shape=tuple(jax.ShapeDtypeStruct(part.shape, f32) for part in (last, prior, parts[2])),
+            in_specs=[anywhere] * 3,
+            out_specs=(hbm,) * 3,
+            scratch_shapes=[dma((cx,))] * 3,
+            compiler_params=pltpu.CompilerParams(vmem_limit_bytes=VMEM_BYTES),
+        )(last, prior, parts[2])
+        return last[None], prior[None], image
 
     in_specs = (
         P("space", None, None),

time: 51.3 us -> 80.6 us (1.57)
  the two profiles are of different devices: /device:TPU:1 before, /device:TPU:0 now
where the time goes in v2:
time: 80.6 us; the launch traced here: 80.4 us
  Pallas kernels  79.8 us (99%)
    pallas_call x1, Pallas kernels, local(): pl.pallas_call(functools.partial(kernel, slabs, shots, steps, (cx, ny, nz...  42.9 us
    pallas_call x1, Pallas kernels, local(): pl.pallas_call(store, out_shape=tuple((jax.ShapeDtypeStruct(part.shape, f...  36.9 us

profile of v2, /device:TPU:0, one launch (start us, length us, event | category | flops | bytes accessed | tf_op | source)
XLA Modules:
  0.0 80.4 jit_solution(6707789814829727518)
XLA Ops:
  0.6 42.9 %shard_map.94 = (f32[1,4,256,128]{3,2,1,0:T(8,128)}, f32[1,4,256,128]{3,2,1,0:T(8,128)}, f32[4,64,128]{2,1,0:T(8,128)}) custom-call(s32[1,384]{1,0:T(1,128)} %bitcast.9, s32[1,384]{1,0:T(1,128)} %cell_hbm.1, f32[3,1,384]{2,1,0:T(1,128)} %bitcast.8, f32[1,4,256,128]{3,2,1,0:T(8,128)} %now_hbm.1, f32[1,4,256,128]{3,2,1,0:T(8,128)} %old_hbm.1, ...), custom_call_target="tpu_custom_call" | custom-call | tf_op jit(solution)/shard_map/pallas_call | solution.py:440
  43.5 36.9 %shard_map.95 = (f32[4,256,128]{2,1,0:T(8,128)}, f32[4,256,128]{2,1,0:T(8,128)}, f32[4,64,128]{2,1,0:T(8,128)}) custom-call(f32[4,256,128]{2,1,0:T(8,128)} %bitcast.6, f32[4,256,128]{2,1,0:T(8,128)} %bitcast.7, f32[4,64,128]{2,1,0:T(8,128)} %get-tuple-element.11.refs_2_), custom_call_target="tpu_custom_call" | custom-call | tf_op jit(solution)/shard_map/pallas_call | solution.py:487

commit v3 on v2

--- a/solution.py
+++ b/solution.py
@@ -92,56 +92,49 @@
             source = now_hbm.at[0, pl.ds(h * half, half), pl.ds(at, rows)]
         else:
             source = ext.at[step, pl.ds(HALO + h * half, half), pl.ds(at + PAD, rows)]
-        lower = me - 3 if up else me - 4
+        if h == 0:
+            target = ext.at[step, pl.ds(0 if up else HALO + cx, half), pl.ds(at + PAD, rows)]
+            arrived, to = diag_recv.at[step, 0, i], me + 1 if up else me - 1
+        else:
+            target = relay_v.at[step * shots + i]
+            arrived, to = relay_recv.at[step * shots + i], me + 4 if up else me - 4
         return pltpu.make_async_remote_copy(
-            src_ref=source,
-            dst_ref=relay_v.at[step * shots + i, 0 if up else 1],
-            send_sem=diag_send.at[step, h, i],
-            recv_sem=relay_recv.at[step * shots + i, 0 if up else 1],
-            device_id=(shot, lower + 7 * h),
+            src_ref=source, dst_ref=target, send_sem=diag_send.at[step, h, i], recv_sem=arrived,
+            device_id=(shot, to), device_id_type=MESH,
+        )
+
+    def relay_copy(g, up):
+        step, i = lax.div(g, shots), lax.rem(g, shots)
+        low_at = (0 if up else HALO + cx) + half
+        return pltpu.make_async_remote_copy(
+            src_ref=relay_v.at[g],
+            dst_ref=ext.at[step, pl.ds(low_at, half), pl.ds(first_row(i) + PAD, rows)],
+            send_sem=relay_send.at[g],
+            recv_sem=diag_recv.at[step, 1, i],
+            device_id=(shot, me - 3 if up else me + 3),
             device_id_type=MESH,
-        )
-
-    def relay_copy(g, up, h):
-        step, i = lax.div(g, shots), lax.rem(g, shots)
-        low_at = (0 if up else HALO + cx) + h * half
-        to = (me + 4 if up else me + 3) - 7 * h
-        return pltpu.make_async_remote_copy(
-            src_ref=relay_v.at[g, 0 if up else 1],
-            dst_ref=ext.at[step, pl.ds(low_at, half), pl.ds(first_row(i) + PAD, rows)],
-            send_sem=relay_send.at[g, 0 if up else 1],
-            recv_sem=diag_recv.at[step, h, i],
-            device_id=(shot, to),
-            device_id_type=MESH,
-        )
-
-    def relay_arrival(g, up):
-        slot = relay_v.at[g, 0 if up else 1]
-        return pltpu.make_async_remote_copy(
-            src_ref=slot, dst_ref=slot,
-            send_sem=relay_send.at[g, 0 if up else 1],
-            recv_sem=relay_recv.at[g, 0 if up else 1],
-            device_id=(shot, me), device_id_type=MESH,
         )
 
     def forward(g):
         if quad:
-            for h, here in ((0, relay_lower), (1, relay_upper)):
+            for up, here in ((False, relay_lower), (True, relay_upper)):
 
                 @pl.when(here)
-                def _(h=h):
-                    for up in (True, False):
-                        relay_arrival(g, up).wait_recv()
-                        relay_copy(g, up, h).start()
+                def _(up=up):
+                    slot = relay_v.at[g]
+                    pltpu.make_async_remote_copy(
+                        src_ref=slot, dst_ref=slot, send_sem=relay_send.at[g], recv_sem=relay_recv.at[g],
+                        device_id=(shot, me), device_id_type=MESH,
+                    ).wait_recv()
+                    relay_copy(g, up).start()
 
     def forwarded(g):
         if quad:
-            for h, here in ((0, relay_lower), (1, relay_upper)):
+            for up, here in ((False, relay_lower), (True, relay_upper)):
 
                 @pl.when(here)
-                def _(h=h):
-                    for up in (True, False):
-                        relay_copy(g, up, h).wait_send()
+                def _(up=up):
+                    relay_copy(g, up).wait_send()
 
     def send_halo(step, i):
         if quad:
@@ -223,13 +216,18 @@
     data_v[steps : steps + 1] = lax.div(cells, nz).astype(jnp.float32)
     data_v[steps + 1 : steps + 2] = lax.rem(cells, nz).astype(jnp.float32)
     slots = lax.broadcasted_iota(jnp.int32, (LANES, count), 0)
+    left, pieces = data_v[...], []
+    for _ in range(3):
+        pieces.append(left.astype(jnp.bfloat16).astype(jnp.float32))
+        left = left - pieces[-1]
+    pieces = jnp.concatenate(pieces, axis=0).astype(jnp.bfloat16)
 
     def pack(d):
-        onehot = jnp.where((slots == lane) & (row == d), 1.0, 0.0)
-        pack_v[d] = lax.dot_general(
-            data_v[...], onehot, (((1,), (1,)), ((), ())),
-            precision=lax.Precision.HIGHEST, preferred_element_type=jnp.float32,
-        )
+        onehot = jnp.where((slots == lane) & (row == d), 1.0, 0.0).astype(jnp.bfloat16)
+        packed = lax.dot_general(
+            pieces, onehot, (((1,), (1,)), ((), ())), preferred_element_type=jnp.float32
+        )
+        pack_v[d] = packed[:PACK] + packed[PACK : 2 * PACK] + packed[2 * PACK :]
 
     def rec_copy(delta):
         to = lax.rem(me + delta, slabs)
@@ -276,6 +274,8 @@
 
     for delta in range(1, slabs):
         rec_arrival(delta).wait_recv()
+    for g in range(1, lead):
+        forward(g)
     flat = cx * ny
     group = 8 if slabs % 8 == 0 else 2
     for step in range(steps):
@@ -307,8 +307,6 @@
             src_v[step] += total[:, step * nz : (step + 1) * nz]
 
     loop(slabs // group, add_sources)
-    for g in range(1, lead):
-        forward(g)
     for copy in (load_now, load_old, load_cour, load_fwd):
         copy.wait()
 
@@ -412,17 +410,20 @@
     loop(shots, lambda i: (out_copy(0, i).wait(), out_copy(1, i).wait()))
 
 
-def store(*refs):
-    count = len(refs) // 3
-    copies = []
+def store(count, *refs):
+    loads, stores = [], []
     for at in range(count):
-        source, target, sems = refs[at], refs[count + at], refs[2 * count + at]
-        for part in range(sems.shape[0]):
-            copies.append(pltpu.make_async_copy(source.at[part], target.at[part], sems.at[part]))
-    for copy in copies:
-        copy.start()
-    for copy in copies:
-        copy.wait()
+        source, target, held, sems = (refs[at + count * kind] for kind in range(4))
+        for part in range(held.shape[0]):
+            loads.append(pltpu.make_async_copy(source.at[part], held.at[part], sems.at[0, part]))
+            stores.append(pltpu.make_async_copy(held.at[part], target.at[part], sems.at[1, part]))
+    for load in loads:
+        load.start()
+    for load, write in zip(loads, stores):
+        load.wait()
+        write.start()
+    for write in stores:
+        write.wait()
 
 
 def solution(mesh):
@@ -462,7 +463,7 @@
                 pltpu.VMEM((shots, cx, rows, nz), f32),
                 pltpu.VMEM((shots, cx, rows, nz), f32),
                 pltpu.VMEM((cx, rows, nz), f32),
-                pltpu.VMEM((steps * shots, 2, cx // 2, rows, nz), f32),
+                pltpu.VMEM((steps * shots, cx // 2, rows, nz), f32),
                 dma((8,)),
                 dma((2, shots)),
                 dma((steps, 2, shots)),
@@ -473,8 +474,8 @@
                 dma((shots,)),
                 dma((steps, 2, shots)),
                 dma((steps, 2, shots)),
-                dma((steps * shots, 2)),
-                dma((steps * shots, 2)),
+                dma((steps * shots,)),
+                dma((steps * shots,)),
             ],
             compiler_params=pltpu.CompilerParams(
                 collective_id=0, has_side_effects=True, vmem_limit_bytes=VMEM_BYTES
@@ -485,11 +486,11 @@
         )
         last, prior = (part.reshape(cx, ny, nz) for part in parts[:2])
         last, prior, image = pl.pallas_call(
-            store,
+            functools.partial(store, 3),
             out_shape=tuple(jax.ShapeDtypeStruct(part.shape, f32) for part in (last, prior, parts[2])),
             in_specs=[anywhere] * 3,
             out_specs=(hbm,) * 3,
-            scratch_shapes=[dma((cx,))] * 3,
+            scratch_shapes=[pltpu.VMEM(part.shape, f32) for part in (last, prior, parts[2])] + [dma((2, cx))] * 3,
             compiler_params=pltpu.CompilerParams(vmem_limit_bytes=VMEM_BYTES),
         )(last, prior, parts[2])
         return last[None], prior[None], image

time: 80.6 us -> 45.4 us (0.56)
  Pallas kernels: 79.8 us -> 43.9 us
    pallas_call x1, Pallas kernels: 36.9 us -> 2.36 us  [local(): pl.pallas_call(functools.partial(store, 3), out_shape=tuple((jax.ShapeDty...]
    pallas_call x1, Pallas kernels: 42.9 us -> 41.6 us  [local(): pl.pallas_call(functools.partial(kernel, slabs, shots, steps, (cx, ny, nz...]
where the time goes in v3:
time: 45.4 us; the launch traced here: 44.6 us
  Pallas kernels  43.9 us (97%)
  between operations  0.64 us (1%)
    pallas_call x1, Pallas kernels, local(): pl.pallas_call(functools.partial(kernel, slabs, shots, steps, (cx, ny, nz...  41.6 us
    pallas_call x1, Pallas kernels, local(): pl.pallas_call(functools.partial(store, 3), out_shape=tuple((jax.ShapeDty...  2.36 us

profile of v3, /device:TPU:0, one launch (start us, length us, event | category | flops | bytes accessed | tf_op | source)
XLA Modules:
  0.0 44.6 jit_solution(2053596408006353435)
XLA Ops:
  0.6 41.6 %shard_map.94 = (f32[1,4,256,128]{3,2,1,0:T(8,128)}, f32[1,4,256,128]{3,2,1,0:T(8,128)}, f32[4,64,128]{2,1,0:T(8,128)}) custom-call(s32[1,384]{1,0:T(1,128)} %bitcast.9, s32[1,384]{1,0:T(1,128)} %cell_hbm.1, f32[3,1,384]{2,1,0:T(1,128)} %bitcast.8, f32[1,4,256,128]{3,2,1,0:T(8,128)} %now_hbm.1, f32[1,4,256,128]{3,2,1,0:T(8,128)} %old_hbm.1, ...), custom_call_target="tpu_custom_call" | custom-call | tf_op jit(solution)/shard_map/pallas_call | solution.py:441
  42.2 2.4 %shard_map.95 = (f32[4,256,128]{2,1,0:T(8,128)}, f32[4,256,128]{2,1,0:T(8,128)}, f32[4,64,128]{2,1,0:T(8,128)}) custom-call(f32[4,256,128]{2,1,0:T(8,128)} %bitcast.6, f32[4,256,128]{2,1,0:T(8,128)} %bitcast.7, f32[4,64,128]{2,1,0:T(8,128)} %get-tuple-element.11.refs_2_), custom_call_target="tpu_custom_call" | custom-call | tf_op jit(solution)/shard_map/pallas_call | solution.py:488

commit v4 on v3

--- a/solution.py
+++ b/solution.py
@@ -335,33 +335,38 @@
 
         def block(b):
             at = pl.multiple_of(start + b * block_rows, block_rows)
+            here = pl.ds(at, block_rows)
+            padded = pl.ds(at + PAD, block_rows)
+            held = pl.ds(pl.multiple_of(b * block_rows, block_rows), block_rows)
+            layers = [ext[step, layer, padded, :] for layer in range(cx + 2 * HALO)]
+            fields, images = [], []
             for x in range(cx):
-                center = ext[step, HALO + x, pl.ds(at + PAD, block_rows), :]
+                center = layers[HALO + x]
                 summed = (3.0 * STENCIL_WEIGHTS[0]) * center
                 for k in range(1, 5):
-                    along = ext[step, HALO + x + k, pl.ds(at + PAD, block_rows), :]
-                    along += ext[step, HALO + x - k, pl.ds(at + PAD, block_rows), :]
-                    along += ext[step, HALO + x, pl.ds(at + PAD + k, block_rows), :]
-                    along += ext[step, HALO + x, pl.ds(at + PAD - k, block_rows), :]
-                    along += jnp.where(z_at < nz - k, pltpu.roll(center, nz - k, 1), 0.0)
-                    along += jnp.where(z_at >= k, pltpu.roll(center, k, 1), 0.0)
-                    summed += STENCIL_WEIGHTS[k] * along
+                    along = layers[HALO + x + k] + layers[HALO + x - k]
+                    beside = ext[step, HALO + x, pl.ds(at + PAD + k, block_rows), :]
+                    beside += ext[step, HALO + x, pl.ds(at + PAD - k, block_rows), :]
+                    deep = jnp.where(z_at < nz - k, pltpu.roll(center, nz - k, 1), 0.0)
+                    deep += jnp.where(z_at >= k, pltpu.roll(center, k, 1), 0.0)
+                    summed += STENCIL_WEIGHTS[k] * (along + beside + deep)
                 if step == 0:
-                    before = old_v[x, pl.ds(at, block_rows), :]
+                    before = old_v[x, here, :]
                 else:
-                    before = ext[step - 1, HALO + x, pl.ds(at + PAD, block_rows), :]
+                    before = ext[step - 1, HALO + x, padded, :]
                 source = src_v[step, pl.ds(pl.multiple_of(x * ny + at, block_rows), block_rows), :]
-                speed = cour_v[x, pl.ds(at, block_rows), :]
-                fresh = 2.0 * center - before + speed * (summed + source)
+                fresh = 2.0 * center - before + cour_v[x, here, :] * (summed + source)
+                image = fwd_v[step, x, here, :].astype(jnp.float32) * fresh
+                if step > 0:
+                    image += img_send[i, x, held, :]
+                fields.append(fresh)
+                images.append(image)
+            for x in range(cx):
                 if step < steps - 1:
-                    ext[step + 1, HALO + x, pl.ds(at + PAD, block_rows), :] = fresh
+                    ext[step + 1, HALO + x, padded, :] = fields[x]
                 else:
-                    last_v[x, pl.ds(at, block_rows), :] = fresh
-                    image = fwd_v[steps - 1, x, pl.ds(at, block_rows), :].astype(jnp.float32) * fresh
-                    for s in range(steps - 1):
-                        field = ext[s + 1, HALO + x, pl.ds(at + PAD, block_rows), :]
-                        image += fwd_v[s, x, pl.ds(at, block_rows), :].astype(jnp.float32) * field
-                    img_send[i, x, pl.ds(pl.multiple_of(b * block_rows, block_rows), block_rows), :] = image
+                    last_v[x, here, :] = fields[x]
+                img_send[i, x, held, :] = images[x]
 
         loop(rows // block_rows, block)
 
@@ -433,7 +438,7 @@
         cx, ny, nz = courant.shape
         steps = residuals.shape[1]
         rows = ny // shots
-        block_rows = min(16, rows)
+        block_rows = min(32, rows)
         anywhere = pl.BlockSpec(memory_space=pl.ANY)
         f32 = jnp.float32
         dma = pltpu.SemaphoreType.DMA

time: 45.4 us -> 45 us (level)
  no operation moved by 1% of the time
where the time goes in v4:
time: 45 us; the launch traced here: 44.2 us
  Pallas kernels  43.5 us (97%)
  between operations  0.64 us (1%)
    pallas_call x1, Pallas kernels, local(): pl.pallas_call(functools.partial(kernel, slabs, shots, steps, (cx, ny, nz...  41.2 us
    pallas_call x1, Pallas kernels, local(): pl.pallas_call(functools.partial(store, 3), out_shape=tuple((jax.ShapeDty...  2.36 us

profile of v4, /device:TPU:0, one launch (start us, length us, event | category | flops | bytes accessed | tf_op | source)
XLA Modules:
  0.0 44.2 jit_solution(9738802941847239102)
XLA Ops:
  0.6 41.2 %shard_map.94 = (f32[1,4,256,128]{3,2,1,0:T(8,128)}, f32[1,4,256,128]{3,2,1,0:T(8,128)}, f32[4,64,128]{2,1,0:T(8,128)}) custom-call(s32[1,384]{1,0:T(1,128)} %bitcast.9, s32[1,384]{1,0:T(1,128)} %cell_hbm.1, f32[3,1,384]{2,1,0:T(1,128)} %bitcast.8, f32[1,4,256,128]{3,2,1,0:T(8,128)} %now_hbm.1, f32[1,4,256,128]{3,2,1,0:T(8,128)} %old_hbm.1, ...), custom_call_target="tpu_custom_call" | custom-call | tf_op jit(solution)/shard_map/pallas_call | solution.py:446
  41.8 2.4 %shard_map.95 = (f32[4,256,128]{2,1,0:T(8,128)}, f32[4,256,128]{2,1,0:T(8,128)}, f32[4,64,128]{2,1,0:T(8,128)}) custom-call(f32[4,256,128]{2,1,0:T(8,128)} %bitcast.6, f32[4,256,128]{2,1,0:T(8,128)} %bitcast.7, f32[4,64,128]{2,1,0:T(8,128)} %get-tuple-element.11.refs_2_), custom_call_target="tpu_custom_call" | custom-call | tf_op jit(solution)/shard_map/pallas_call | solution.py:493

commit v5 on v4

--- a/solution.py
+++ b/solution.py
@@ -21,7 +21,7 @@
     slabs, shots, steps, extent, block_rows,
     slab_hbm, cell_hbm, res_hbm, now_hbm, old_hbm, cour_hbm, fwd_hbm,
     last_hbm, prior_hbm, image_hbm,
-    slab_ref, cell_ref, res_ref, ext, old_v, cour_v, fwd_v, last_v, src_v, data_v, pack_v, got_v, img_send, img_recv, image_ref, relay_v,
+    slab_ref, cell_ref, res_ref, ext, old_v, cour_v, fwd_v, last_v, src_v, held_v, piece_v, data_v, pack_v, got_v, img_send, img_recv, image_ref, relay_v,
     load_sem, out_sem, halo_send, halo_recv, rec_send, rec_recv, img_ssem, img_rsem,
     diag_send, diag_recv, relay_send, relay_recv,
 ):
@@ -276,37 +276,32 @@
         rec_arrival(delta).wait_recv()
     for g in range(1, lead):
         forward(g)
-    flat = cx * ny
-    group = 8 if slabs % 8 == 0 else 2
-    for step in range(steps):
-        src_v[step] = jnp.zeros((flat, nz), jnp.float32)
-
-    def add_sources(g):
-        held = jnp.concatenate(
-            [got_v[g * group + 2 * p] + got_v[g * group + 2 * p + 1] for p in range(group // 2)], axis=1
-        )
-        where_row = held[steps : steps + 1].astype(jnp.int32)
-        where_lane = held[steps + 1 : steps + 2].astype(jnp.int32)
-        width = held.shape[1]
-        picks = jnp.where(
-            lax.broadcasted_iota(jnp.int32, (flat, width), 0) == where_row, 1.0, 0.0
-        ).astype(jnp.bfloat16)
+    for p in range(slabs // 2):
+        held_v[:, p * LANES : (p + 1) * LANES] = got_v[2 * p] + got_v[2 * p + 1]
+    width = slabs // 2 * LANES
+
+    def place_sources(step):
+        where_lane = held_v[steps + 1 : steps + 2].astype(jnp.int32)
         hits = lax.broadcasted_iota(jnp.int32, (nz, width), 0) == where_lane
-        rest = jnp.concatenate(
-            [jnp.where(hits, held[step : step + 1], 0.0) for step in range(steps)], axis=0
-        )
-        total = None
-        for _ in range(3):
+        rest = jnp.where(hits, held_v[step : step + 1], 0.0)
+        for p in range(3):
             piece = rest.astype(jnp.bfloat16)
             rest = rest - piece.astype(jnp.float32)
-            term = lax.dot_general(
-                picks, piece, (((1,), (1,)), ((), ())), preferred_element_type=jnp.float32
-            )
-            total = term if total is None else total + term
-        for step in range(steps):
-            src_v[step] += total[:, step * nz : (step + 1) * nz]
-
-    loop(slabs // group, add_sources)
+            piece_v[p] = piece
+
+    def add_sources(i):
+        where_row = held_v[steps : steps + 1].astype(jnp.int32) - first_row(i)
+        within = lax.broadcasted_iota(jnp.int32, (rows, width), 0)
+        for x in range(cx):
+            picks = jnp.where(within + x * ny == where_row, 1.0, 0.0).astype(jnp.bfloat16)
+            total = None
+            for p in range(3):
+                term = lax.dot_general(
+                    picks, piece_v[p], (((1,), (1,)), ((), ())), preferred_element_type=jnp.float32
+                )
+                total = term if total is None else total + term
+            src_v[x] = total
+
     for copy in (load_now, load_old, load_cour, load_fwd):
         copy.wait()
 
@@ -354,7 +349,7 @@
                     before = old_v[x, here, :]
                 else:
                     before = ext[step - 1, HALO + x, padded, :]
-                source = src_v[step, pl.ds(pl.multiple_of(x * ny + at, block_rows), block_rows), :]
+                source = src_v[x, held, :]
                 fresh = 2.0 * center - before + cour_v[x, here, :] * (summed + source)
                 image = fwd_v[step, x, here, :].astype(jnp.float32) * fresh
                 if step > 0:
@@ -371,6 +366,7 @@
         loop(rows // block_rows, block)
 
     for step in range(steps):
+        place_sources(step)
 
         def chunk(i, step=step):
             ahead = step * shots + i + lead
@@ -379,6 +375,7 @@
             def _():
                 forward(ahead)
 
+            add_sources(i)
             wait_halo(step, i)
             update(step, i)
             if step < steps - 1:
@@ -461,7 +458,9 @@
                 pltpu.VMEM((cx, ny, nz), f32),
                 pltpu.VMEM(forward.shape[1:], forward.dtype),
                 pltpu.VMEM((cx, ny, nz), f32),
-                pltpu.VMEM((steps, cx * ny, nz), f32),
+                pltpu.VMEM((cx, rows, nz), f32),
+                pltpu.VMEM((PACK, slabs // 2 * LANES), f32),
+                pltpu.VMEM((3, nz, slabs // 2 * LANES), jnp.bfloat16),
                 pltpu.VMEM((PACK, receiver_cell.shape[1]), f32),
                 pltpu.VMEM((slabs, PACK, LANES), f32),
                 pltpu.VMEM((slabs, PACK, LANES), f32),

time: 45 us -> 45.1 us (level)
  no operation moved by 1% of the time
where the time goes in v5:
time: 45.1 us; the launch traced here: 44.4 us
  Pallas kernels  43.7 us (97%)
  between operations  0.64 us (1%)
    pallas_call x1, Pallas kernels, local(): pl.pallas_call(functools.partial(kernel, slabs, shots, steps, (cx, ny, nz...  41.4 us
    pallas_call x1, Pallas kernels, local(): pl.pallas_call(functools.partial(store, 3), out_shape=tuple((jax.ShapeDty...  2.36 us

profile of v5, /device:TPU:0, one launch (start us, length us, event | category | flops | bytes accessed | tf_op | source)
XLA Modules:
  0.0 44.4 jit_solution(15107544820713282661)
XLA Ops:
  0.6 41.4 %shard_map.94 = (f32[1,4,256,128]{3,2,1,0:T(8,128)}, f32[1,4,256,128]{3,2,1,0:T(8,128)}, f32[4,64,128]{2,1,0:T(8,128)}) custom-call(s32[1,384]{1,0:T(1,128)} %bitcast.9, s32[1,384]{1,0:T(1,128)} %cell_hbm.1, f32[3,1,384]{2,1,0:T(1,128)} %bitcast.8, f32[1,4,256,128]{3,2,1,0:T(8,128)} %now_hbm.1, f32[1,4,256,128]{3,2,1,0:T(8,128)} %old_hbm.1, ...), custom_call_target="tpu_custom_call" | custom-call | tf_op jit(solution)/shard_map/pallas_call | solution.py:443
  42.0 2.4 %shard_map.95 = (f32[4,256,128]{2,1,0:T(8,128)}, f32[4,256,128]{2,1,0:T(8,128)}, f32[4,64,128]{2,1,0:T(8,128)}) custom-call(f32[4,256,128]{2,1,0:T(8,128)} %bitcast.6, f32[4,256,128]{2,1,0:T(8,128)} %bitcast.7, f32[4,64,128]{2,1,0:T(8,128)} %get-tuple-element.11.refs_2_), custom_call_target="tpu_custom_call" | custom-call | tf_op jit(solution)/shard_map/pallas_call | solution.py:492

commit v6 on v5

--- a/solution.py
+++ b/solution.py
@@ -137,14 +137,6 @@
                     relay_copy(g, up).wait_send()
 
     def send_halo(step, i):
-        if quad:
-            for up, here in ((False, diag_low), (True, diag_high)):
-
-                @pl.when(here)
-                def _(up=up):
-                    for h in range(2):
-                        diag_copy(step, i, up, h).start()
-
         @pl.when(near_low)
         def _():
             halo_copy(step, i, 0).start()
@@ -152,6 +144,14 @@
         @pl.when(near_high)
         def _():
             halo_copy(step, i, 1).start()
+
+        if quad:
+            for up, here in ((False, diag_low), (True, diag_high)):
+
+                @pl.when(here)
+                def _(up=up):
+                    for h in (1, 0):
+                        diag_copy(step, i, up, h).start()
 
     def wait_halo(step, i):
         @pl.when(near_high)
@@ -369,12 +369,6 @@
         place_sources(step)
 
         def chunk(i, step=step):
-            ahead = step * shots + i + lead
-
-            @pl.when(ahead < steps * shots)
-            def _():
-                forward(ahead)
-
             add_sources(i)
             wait_halo(step, i)
             update(step, i)
@@ -388,6 +382,12 @@
                 @pl.when(i < shots - 1)
                 def _():
                     img_copy(i).start()
+
+            ahead = step * shots + i + 1
+
+            @pl.when((ahead >= lead) & (ahead < steps * shots))
+            def _():
+                forward(ahead)
 
         loop(shots, chunk)
 

time: 45.1 us -> 44.1 us (0.978)
  the two profiles are of different devices: /device:TPU:0 before, /device:TPU:11 now
where the time goes in v6:
time: 44.1 us; the launch traced here: 43.9 us
  Pallas kernels  43.3 us (98%)
  between operations  0.64 us (1%)
    pallas_call x1, Pallas kernels, local(): pl.pallas_call(functools.partial(kernel, slabs, shots, steps, (cx, ny, nz...  40.9 us
    pallas_call x1, Pallas kernels, local(): pl.pallas_call(functools.partial(store, 3), out_shape=tuple((jax.ShapeDty...  2.36 us

profile of v6, /device:TPU:11, one launch (start us, length us, event | category | flops | bytes accessed | tf_op | source)
XLA Modules:
  0.0 43.9 jit_solution(13892427938139773615)
XLA Ops:
  0.6 40.9 %shard_map.94 = (f32[1,4,256,128]{3,2,1,0:T(8,128)}, f32[1,4,256,128]{3,2,1,0:T(8,128)}, f32[4,64,128]{2,1,0:T(8,128)}) custom-call(s32[1,384]{1,0:T(1,128)} %bitcast.9, s32[1,384]{1,0:T(1,128)} %cell_hbm.1, f32[3,1,384]{2,1,0:T(1,128)} %bitcast.8, f32[1,4,256,128]{3,2,1,0:T(8,128)} %now_hbm.1, f32[1,4,256,128]{3,2,1,0:T(8,128)} %old_hbm.1, ...), custom_call_target="tpu_custom_call" | custom-call | tf_op jit(solution)/shard_map/pallas_call | solution.py:443
  41.6 2.4 %shard_map.95 = (f32[4,256,128]{2,1,0:T(8,128)}, f32[4,256,128]{2,1,0:T(8,128)}, f32[4,64,128]{2,1,0:T(8,128)}) custom-call(f32[4,256,128]{2,1,0:T(8,128)} %bitcast.6, f32[4,256,128]{2,1,0:T(8,128)} %bitcast.7, f32[4,64,128]{2,1,0:T(8,128)} %get-tuple-element.11.refs_2_), custom_call_target="tpu_custom_call" | custom-call | tf_op jit(solution)/shard_map/pallas_call | solution.py:492

commit v7 on v6

--- a/solution.py
+++ b/solution.py
@@ -21,9 +21,9 @@
     slabs, shots, steps, extent, block_rows,
     slab_hbm, cell_hbm, res_hbm, now_hbm, old_hbm, cour_hbm, fwd_hbm,
     last_hbm, prior_hbm, image_hbm,
-    slab_ref, cell_ref, res_ref, ext, old_v, cour_v, fwd_v, last_v, src_v, held_v, piece_v, data_v, pack_v, got_v, img_send, img_recv, image_ref, relay_v,
+    slab_ref, cell_ref, res_ref, ext, old_v, cour_v, fwd_v, last_v, src_v, held_v, piece_v, data_v, pack_v, got_v, img_send, img_recv, pre_v, image_ref, relay_v,
     load_sem, out_sem, halo_send, halo_recv, rec_send, rec_recv, img_ssem, img_rsem,
-    diag_send, diag_recv, relay_send, relay_recv,
+    diag_send, diag_recv, relay_send, relay_recv, pre_rsem,
 ):
     cx, ny, nz = extent
     rows = ny // shots
@@ -56,8 +56,21 @@
         )
     pl.semaphore_wait(barrier, slabs - 1 + shots - 1)
 
+    def target_shot(i):
+        if shots & (shots - 1):
+            return lax.rem(shot + 1 + i, shots)
+        flips, target, bit = shots - 1 - i, 0, 1
+        while bit < shots:
+            target += lax.rem(lax.div(shot, bit) + lax.div(flips, bit), 2) * bit
+            bit *= 2
+        return target
+
+    line = shots == 4
+    outer = (shot == 0) | (shot == shots - 1)
+    inner = (shot != 0) & (shot != shots - 1)
+
     def first_row(i):
-        return pl.multiple_of(lax.rem(shot + 1 + i, shots) * rows, rows)
+        return pl.multiple_of(target_shot(i) * rows, rows)
 
     def halo_copy(step, i, side):
         at = first_row(i)
@@ -261,6 +274,13 @@
             for layer in range(HALO):
                 ext[step, low_at + layer] = jnp.zeros((ny + 2 * PAD, nz), jnp.float32)
 
+    if line:
+
+        @pl.when(outer)
+        def _():
+            for x in range(cx):
+                img_recv[0, x] = jnp.zeros((rows, nz), jnp.float32)
+
     @pl.when(me == 0)
     def _():
         clear(0)
@@ -309,7 +329,13 @@
         return pltpu.make_async_remote_copy(
             src_ref=img_send.at[i], dst_ref=img_recv.at[i],
             send_sem=img_ssem.at[i], recv_sem=img_rsem.at[i],
-            device_id=(lax.rem(shot + 1 + i, shots), me), device_id_type=MESH,
+            device_id=(target_shot(i), me), device_id_type=MESH,
+        )
+
+    def pre_copy():
+        return pltpu.make_async_remote_copy(
+            src_ref=img_send.at[0], dst_ref=pre_v, send_sem=img_ssem.at[0], recv_sem=pre_rsem.at[0],
+            device_id=(shot + 1 - 2 * lax.rem(shot, 2), me), device_id_type=MESH,
         )
 
     def out_copy(which, i):
@@ -379,9 +405,28 @@
             if step == steps - 1:
                 out_copy(0, i).start()
 
-                @pl.when(i < shots - 1)
-                def _():
-                    img_copy(i).start()
+                if line:
+
+                    @pl.when((outer & (i > 0) & (i < shots - 1)) | (inner & ((i == 0) | (i == 2))))
+                    def _():
+                        img_copy(i).start()
+
+                    @pl.when(outer & (i == 0))
+                    def _():
+                        pre_copy().start()
+
+                    @pl.when(inner & (i == 2))
+                    def _():
+                        pre_copy().wait_recv()
+                        for x in range(cx):
+                            img_send[1, x] += pre_v[x]
+                        img_copy(1).start()
+
+                else:
+
+                    @pl.when(i < shots - 1)
+                    def _():
+                        img_copy(i).start()
 
             ahead = step * shots + i + 1
 
@@ -391,7 +436,13 @@
 
         loop(shots, chunk)
 
-    for i in range(shots - 1):
+    if line:
+
+        @pl.when(inner)
+        def _():
+            img_copy(0).wait_recv()
+
+    for i in range(1 if line else 0, shots - 1):
         img_copy(i).wait_recv()
     for x in range(cx):
         total = img_send[shots - 1, x]
@@ -405,7 +456,17 @@
         loop(shots, lambda i, step=step: wait_sent(step, i))
     for delta in range(1, slabs):
         rec_copy(delta).wait_send()
-    for i in range(shots - 1):
+    if line:
+
+        @pl.when(outer)
+        def _():
+            pre_copy().wait_send()
+
+        @pl.when(inner)
+        def _():
+            img_copy(0).wait_send()
+
+    for i in range(1 if line else 0, shots - 1):
         img_copy(i).wait_send()
     loop(steps * shots, forwarded)
     image_out.wait()
@@ -467,6 +528,7 @@
                 pltpu.VMEM((shots, cx, rows, nz), f32),
                 pltpu.VMEM((shots, cx, rows, nz), f32),
                 pltpu.VMEM((cx, rows, nz), f32),
+                pltpu.VMEM((cx, rows, nz), f32),
                 pltpu.VMEM((steps * shots, cx // 2, rows, nz), f32),
                 dma((8,)),
                 dma((2, shots)),
@@ -480,6 +542,7 @@
                 dma((steps, 2, shots)),
                 dma((steps * shots,)),
                 dma((steps * shots,)),
+                dma((1,)),
             ],
             compiler_params=pltpu.CompilerParams(
                 collective_id=0, has_side_effects=True, vmem_limit_bytes=VMEM_BYTES

time: 44.1 us -> 42.6 us (0.966)
  the two profiles are of different devices: /device:TPU:11 before, /device:TPU:5 now
where the time goes in v7:
time: 42.6 us; the launch traced here: 42.4 us
  Pallas kernels  41.8 us (98%)
  between operations  0.64 us (2%)
    pallas_call x1, Pallas kernels, local(): pl.pallas_call(functools.partial(kernel, slabs, shots, steps, (cx, ny, nz...  39.4 us
    pallas_call x1, Pallas kernels, local(): pl.pallas_call(functools.partial(store, 3), out_shape=tuple((jax.ShapeDty...  2.36 us

profile of v7, /device:TPU:5, one launch (start us, length us, event | category | flops | bytes accessed | tf_op | source)
XLA Modules:
  0.0 42.4 jit_solution(10770498974935378110)
XLA Ops:
  0.6 39.4 %shard_map.94 = (f32[1,4,256,128]{3,2,1,0:T(8,128)}, f32[1,4,256,128]{3,2,1,0:T(8,128)}, f32[4,64,128]{2,1,0:T(8,128)}) custom-call(s32[1,384]{1,0:T(1,128)} %bitcast.9, s32[1,384]{1,0:T(1,128)} %cell_hbm.1, f32[3,1,384]{2,1,0:T(1,128)} %bitcast.8, f32[1,4,256,128]{3,2,1,0:T(8,128)} %now_hbm.1, f32[1,4,256,128]{3,2,1,0:T(8,128)} %old_hbm.1, ...), custom_call_target="tpu_custom_call" | custom-call | tf_op jit(solution)/shard_map/pallas_call | solution.py:504
  40.1 2.4 %shard_map.95 = (f32[4,256,128]{2,1,0:T(8,128)}, f32[4,256,128]{2,1,0:T(8,128)}, f32[4,64,128]{2,1,0:T(8,128)}) custom-call(f32[4,256,128]{2,1,0:T(8,128)} %bitcast.6, f32[4,256,128]{2,1,0:T(8,128)} %bitcast.7, f32[4,64,128]{2,1,0:T(8,128)} %get-tuple-element.11.refs_2_), custom_call_target="tpu_custom_call" | custom-call | tf_op jit(solution)/shard_map/pallas_call | solution.py:555

commit v8 on v7

--- a/solution.py
+++ b/solution.py
@@ -27,6 +27,8 @@
 ):
     cx, ny, nz = extent
     rows = ny // shots
+    sub = 2 if rows % 64 == 0 else 1
+    chunks, strip = shots * sub, rows // sub
     me = lax.axis_index("space")
     shot = lax.axis_index("shot")
 
@@ -70,18 +72,18 @@
     inner = (shot != 0) & (shot != shots - 1)
 
     def first_row(i):
-        return pl.multiple_of(target_shot(i) * rows, rows)
+        return pl.multiple_of(target_shot(lax.div(i, sub)) * rows + lax.rem(i, sub) * strip, strip)
 
     def halo_copy(step, i, side):
         at = first_row(i)
         if step == 0:
-            source = now_hbm.at[0, :, pl.ds(at, rows)]
+            source = now_hbm.at[0, :, pl.ds(at, strip)]
         else:
-            source = ext.at[step, pl.ds(HALO, cx), pl.ds(at + PAD, rows)]
+            source = ext.at[step, pl.ds(HALO, cx), pl.ds(at + PAD, strip)]
         low_at = HALO + cx if side == 0 else 0
         return pltpu.make_async_remote_copy(
             src_ref=source,
-            dst_ref=ext.at[step, pl.ds(low_at, HALO), pl.ds(at + PAD, rows)],
+            dst_ref=ext.at[step, pl.ds(low_at, HALO), pl.ds(at + PAD, strip)],
             send_sem=halo_send.at[step, side, i],
             recv_sem=halo_recv.at[step, side, i],
             device_id=(shot, me - 1 if side == 0 else me + 1),
@@ -102,26 +104,26 @@
     def diag_copy(step, i, up, h):
         at = first_row(i)
         if step == 0:
-            source = now_hbm.at[0, pl.ds(h * half, half), pl.ds(at, rows)]
+            source = now_hbm.at[0, pl.ds(h * half, half), pl.ds(at, strip)]
         else:
-            source = ext.at[step, pl.ds(HALO + h * half, half), pl.ds(at + PAD, rows)]
+            source = ext.at[step, pl.ds(HALO + h * half, half), pl.ds(at + PAD, strip)]
         if h == 0:
-            target = ext.at[step, pl.ds(0 if up else HALO + cx, half), pl.ds(at + PAD, rows)]
+            target = ext.at[step, pl.ds(0 if up else HALO + cx, half), pl.ds(at + PAD, strip)]
             arrived, to = diag_recv.at[step, 0, i], me + 1 if up else me - 1
         else:
-            target = relay_v.at[step * shots + i]
-            arrived, to = relay_recv.at[step * shots + i], me + 4 if up else me - 4
+            target = relay_v.at[step * chunks + i]
+            arrived, to = relay_recv.at[step * chunks + i], me + 4 if up else me - 4
         return pltpu.make_async_remote_copy(
             src_ref=source, dst_ref=target, send_sem=diag_send.at[step, h, i], recv_sem=arrived,
             device_id=(shot, to), device_id_type=MESH,
         )
 
     def relay_copy(g, up):
-        step, i = lax.div(g, shots), lax.rem(g, shots)
+        step, i = lax.div(g, chunks), lax.rem(g, chunks)
         low_at = (0 if up else HALO + cx) + half
         return pltpu.make_async_remote_copy(
             src_ref=relay_v.at[g],
-            dst_ref=ext.at[step, pl.ds(low_at, half), pl.ds(first_row(i) + PAD, rows)],
+            dst_ref=ext.at[step, pl.ds(low_at, half), pl.ds(first_row(i) + PAD, strip)],
             send_sem=relay_send.at[g],
             recv_sem=diag_recv.at[step, 1, i],
             device_id=(shot, me - 3 if up else me + 3),
@@ -182,7 +184,7 @@
                 def _(up=up):
                     for h in range(2):
                         low_at = (0 if up else HALO + cx) + h * half
-                        slot = ext.at[step, pl.ds(low_at, half), pl.ds(first_row(i) + PAD, rows)]
+                        slot = ext.at[step, pl.ds(low_at, half), pl.ds(first_row(i) + PAD, strip)]
                         pltpu.make_async_remote_copy(
                             src_ref=slot, dst_ref=slot,
                             send_sem=diag_send.at[step, h, i],
@@ -261,7 +263,7 @@
     loop(slabs, pack)
     for delta in range(1, slabs):
         rec_copy(delta).start()
-    loop(shots - 1, lambda i: send_halo(0, i + 1))
+    loop(chunks - 1, lambda i: send_halo(0, i + 1))
     got_v[me] = pack_v[me]
 
     edge = jnp.zeros((cx, PAD, nz), jnp.float32)
@@ -289,7 +291,7 @@
     def _():
         clear(HALO + cx)
 
-    lead = shots // 2
+    lead = chunks // 2
     forward(0)
 
     for delta in range(1, slabs):
@@ -311,7 +313,7 @@
 
     def add_sources(i):
         where_row = held_v[steps : steps + 1].astype(jnp.int32) - first_row(i)
-        within = lax.broadcasted_iota(jnp.int32, (rows, width), 0)
+        within = lax.broadcasted_iota(jnp.int32, (strip, width), 0)
         for x in range(cx):
             picks = jnp.where(within + x * ny == where_row, 1.0, 0.0).astype(jnp.bfloat16)
             total = None
@@ -342,23 +344,25 @@
         at = first_row(i)
         if which == 0:
             return pltpu.make_async_copy(
-                last_v.at[:, pl.ds(at, rows)], last_hbm.at[0, :, pl.ds(at, rows)], out_sem.at[0, i]
+                last_v.at[:, pl.ds(at, strip)], last_hbm.at[0, :, pl.ds(at, strip)], out_sem.at[0, i]
             )
         return pltpu.make_async_copy(
-            ext.at[steps - 1, pl.ds(HALO, cx), pl.ds(at + PAD, rows)],
-            prior_hbm.at[0, :, pl.ds(at, rows)], out_sem.at[1, i],
+            ext.at[steps - 1, pl.ds(HALO, cx), pl.ds(at + PAD, strip)],
+            prior_hbm.at[0, :, pl.ds(at, strip)], out_sem.at[1, i],
         )
 
     z_at = lax.broadcasted_iota(jnp.int32, (block_rows, nz), 1)
 
     def update(step, i):
         start = first_row(i)
+        slot, base = lax.div(i, sub), lax.rem(i, sub) * strip
 
         def block(b):
             at = pl.multiple_of(start + b * block_rows, block_rows)
             here = pl.ds(at, block_rows)
             padded = pl.ds(at + PAD, block_rows)
-            held = pl.ds(pl.multiple_of(b * block_rows, block_rows), block_rows)
+            held = pl.ds(pl.multiple_of(base + b * block_rows, block_rows), block_rows)
+            local = pl.ds(pl.multiple_of(b * block_rows, block_rows), block_rows)
             layers = [ext[step, layer, padded, :] for layer in range(cx + 2 * HALO)]
             fields, images = [], []
             for x in range(cx):
@@ -375,11 +379,11 @@
                     before = old_v[x, here, :]
                 else:
                     before = ext[step - 1, HALO + x, padded, :]
-                source = src_v[x, held, :]
+                source = src_v[x, local, :]
                 fresh = 2.0 * center - before + cour_v[x, here, :] * (summed + source)
                 image = fwd_v[step, x, here, :].astype(jnp.float32) * fresh
                 if step > 0:
-                    image += img_send[i, x, held, :]
+                    image += img_send[slot, x, held, :]
                 fields.append(fresh)
                 images.append(image)
             for x in range(cx):
@@ -387,14 +391,15 @@
                     ext[step + 1, HALO + x, padded, :] = fields[x]
                 else:
                     last_v[x, here, :] = fields[x]
-                img_send[i, x, held, :] = images[x]
-
-        loop(rows // block_rows, block)
+                img_send[slot, x, held, :] = images[x]
+
+        loop(strip // block_rows, block)
 
     for step in range(steps):
         place_sources(step)
 
         def chunk(i, step=step):
+            ahead = step * chunks + i + 1
             add_sources(i)
             wait_halo(step, i)
             update(step, i)
@@ -405,17 +410,19 @@
             if step == steps - 1:
                 out_copy(0, i).start()
 
+                done = lax.rem(i, sub) == sub - 1
+                i = lax.div(i, sub)
                 if line:
 
-                    @pl.when((outer & (i > 0) & (i < shots - 1)) | (inner & ((i == 0) | (i == 2))))
+                    @pl.when(done & ((outer & (i > 0) & (i < shots - 1)) | (inner & ((i == 0) | (i == 2)))))
                     def _():
                         img_copy(i).start()
 
-                    @pl.when(outer & (i == 0))
+                    @pl.when(done & outer & (i == 0))
                     def _():
                         pre_copy().start()
 
-                    @pl.when(inner & (i == 2))
+                    @pl.when(done & inner & (i == 2))
                     def _():
                         pre_copy().wait_recv()
                         for x in range(cx):
@@ -424,17 +431,16 @@
 
                 else:
 
-                    @pl.when(i < shots - 1)
+                    @pl.when(done & (i < shots - 1))
                     def _():
                         img_copy(i).start()
 
-            ahead = step * shots + i + 1
-
-            @pl.when((ahead >= lead) & (ahead < steps * shots))
+
+            @pl.when((ahead >= lead) & (ahead < steps * chunks))
             def _():
                 forward(ahead)
 
-        loop(shots, chunk)
+        loop(chunks, chunk)
 
     if line:
 
@@ -453,7 +459,7 @@
     image_out.start()
 
     for step in range(steps):
-        loop(shots, lambda i, step=step: wait_sent(step, i))
+        loop(chunks, lambda i, step=step: wait_sent(step, i))
     for delta in range(1, slabs):
         rec_copy(delta).wait_send()
     if line:
@@ -468,9 +474,9 @@
 
     for i in range(1 if line else 0, shots - 1):
         img_copy(i).wait_send()
-    loop(steps * shots, forwarded)
+    loop(steps * chunks, forwarded)
     image_out.wait()
-    loop(shots, lambda i: (out_copy(0, i).wait(), out_copy(1, i).wait()))
+    loop(chunks, lambda i: (out_copy(0, i).wait(), out_copy(1, i).wait()))
 
 
 def store(count, *refs):
@@ -496,7 +502,9 @@
         cx, ny, nz = courant.shape
         steps = residuals.shape[1]
         rows = ny // shots
-        block_rows = min(32, rows)
+        sub = 2 if rows % 64 == 0 else 1
+        chunks, strip = shots * sub, rows // sub
+        block_rows = min(32, strip)
         anywhere = pl.BlockSpec(memory_space=pl.ANY)
         f32 = jnp.float32
         dma = pltpu.SemaphoreType.DMA
@@ -519,7 +527,7 @@
                 pltpu.VMEM((cx, ny, nz), f32),
                 pltpu.VMEM(forward.shape[1:], forward.dtype),
                 pltpu.VMEM((cx, ny, nz), f32),
-                pltpu.VMEM((cx, rows, nz), f32),
+                pltpu.VMEM((cx, strip, nz), f32),
                 pltpu.VMEM((PACK, slabs // 2 * LANES), f32),
                 pltpu.VMEM((3, nz, slabs // 2 * LANES), jnp.bfloat16),
                 pltpu.VMEM((PACK, receiver_cell.shape[1]), f32),
@@ -529,19 +537,19 @@
                 pltpu.VMEM((shots, cx, rows, nz), f32),
                 pltpu.VMEM((cx, rows, nz), f32),
                 pltpu.VMEM((cx, rows, nz), f32),
-                pltpu.VMEM((steps * shots, cx // 2, rows, nz), f32),
+                pltpu.VMEM((steps * chunks, cx // 2, strip, nz), f32),
                 dma((8,)),
-                dma((2, shots)),
-                dma((steps, 2, shots)),
-                dma((steps, 2, shots)),
+                dma((2, chunks)),
+                dma((steps, 2, chunks)),
+                dma((steps, 2, chunks)),
                 dma((slabs,)),
                 dma((slabs,)),
                 dma((shots,)),
                 dma((shots,)),
-                dma((steps, 2, shots)),
-                dma((steps, 2, shots)),
-                dma((steps * shots,)),
-                dma((steps * shots,)),
+                dma((steps, 2, chunks)),
+                dma((steps, 2, chunks)),
+                dma((steps * chunks,)),
+                dma((steps * chunks,)),
                 dma((1,)),
             ],
             compiler_params=pltpu.CompilerParams(

time: 42.6 us -> 43.9 us (1.031)
  the two profiles are of different devices: /device:TPU:5 before, /device:TPU:1 now
where the time goes in v8:
time: 43.9 us; the launch traced here: 43.7 us
  Pallas kernels  43.1 us (98%)
  between operations  0.64 us (1%)
    pallas_call x1, Pallas kernels, local(): pl.pallas_call(functools.partial(kernel, slabs, shots, steps, (cx, ny, nz...  40.7 us
    pallas_call x1, Pallas kernels, local(): pl.pallas_call(functools.partial(store, 3), out_shape=tuple((jax.ShapeDty...  2.36 us

profile of v8, /device:TPU:1, one launch (start us, length us, event | category | flops | bytes accessed | tf_op | source)
XLA Modules:
  0.0 43.7 jit_solution(4942456378257223509)
XLA Ops:
  0.6 40.7 %shard_map.94 = (f32[1,4,256,128]{3,2,1,0:T(8,128)}, f32[1,4,256,128]{3,2,1,0:T(8,128)}, f32[4,64,128]{2,1,0:T(8,128)}) custom-call(s32[1,384]{1,0:T(1,128)} %bitcast.9, s32[1,384]{1,0:T(1,128)} %cell_hbm.1, f32[3,1,384]{2,1,0:T(1,128)} %bitcast.8, f32[1,4,256,128]{3,2,1,0:T(8,128)} %now_hbm.1, f32[1,4,256,128]{3,2,1,0:T(8,128)} %old_hbm.1, ...), custom_call_target="tpu_custom_call" | custom-call | tf_op jit(solution)/shard_map/pallas_call | solution.py:512
  41.4 2.4 %shard_map.95 = (f32[4,256,128]{2,1,0:T(8,128)}, f32[4,256,128]{2,1,0:T(8,128)}, f32[4,64,128]{2,1,0:T(8,128)}) custom-call(f32[4,256,128]{2,1,0:T(8,128)} %bitcast.6, f32[4,256,128]{2,1,0:T(8,128)} %bitcast.7, f32[4,64,128]{2,1,0:T(8,128)} %get-tuple-element.11.refs_2_), custom_call_target="tpu_custom_call" | custom-call | tf_op jit(solution)/shard_map/pallas_call | solution.py:563
